TPU v7x, 32 devices: a whole 2x2x4 slice. The times are simulated.
32 devices in a mesh: fsdp: 8 (over z, y), tp: 4 (over x, core).
Axes of the slice: x: 2, y: 2, z: 4, core: 2. Of those that a mesh axis runs over, the one named last changes fastest.
Arguments:
- tokens: bfloat16 [16384, 1024], P(('fsdp', 'tp')), may hold values from -6 to 6
- positions: int32 [16384], P('fsdp'), may hold values from 0 to 3069, as said below
- first_gain: float32 [1024], replicated, may hold values from 0.25 to 1.75
- query_weight: bfloat16 [1024, 1024], P('fsdp', 'tp'), may hold values from -0.1875 to 0.1875
- key_weight: bfloat16 [1024, 512], P('fsdp', 'tp'), may hold values from -0.1875 to 0.1875
- value_weight: bfloat16 [1024, 512], P('fsdp', 'tp'), may hold values from -0.1875 to 0.1875
- query_gain: float32 [64], replicated, may hold values from 0.25 to 1.75
- key_gain: float32 [64], replicated, may hold values from 0.25 to 1.75
- out_weight: bfloat16 [1024, 1024], P('tp', 'fsdp'), may hold values from -2 to 2
- second_gain: float32 [1024], replicated, may hold values from 0.25 to 1.75
- gate_weight: bfloat16 [1024, 4608], P('fsdp', 'tp'), may hold values from -0.1875 to 0.1875
- up_weight: bfloat16 [1024, 4608], P('fsdp', 'tp'), may hold values from -0.1875 to 0.1875
- down_weight: bfloat16 [4608, 1024], P('tp', 'fsdp'), may hold values from -0.09375 to 0.09375
- cotangent: bfloat16 [16384, 1024], P(('fsdp', 'tp')), may hold values from -6 to 6
Outputs:
- output: bfloat16 [16384, 1024], P(('fsdp', 'tp'))
- grad_tokens: float32 [16384, 1024], P(('fsdp', 'tp'))
- grad_first_gain: float32 [1024], replicated
- grad_query_weight: float32 [1024, 1024], P('fsdp', 'tp')
- grad_key_weight: float32 [1024, 512], P('fsdp', 'tp')
- grad_value_weight: float32 [1024, 512], P('fsdp', 'tp')
- grad_query_gain: float32 [64], replicated
- grad_key_gain: float32 [64], replicated
- grad_out_weight: float32 [1024, 1024], P('tp', 'fsdp')
- grad_second_gain: float32 [1024], replicated
- grad_gate_weight: float32 [1024, 4608], P('fsdp', 'tp')
- grad_up_weight: float32 [1024, 4608], P('fsdp', 'tp')
- grad_down_weight: float32 [4608, 1024], P('tp', 'fsdp')
Inputs may be any that keep to these rules, and one draw needn't show every extreme that they name: Within each sequence of 1024 consecutive tokens the positions start at 0 and rise by 1 to 3 from each token to the next; in some sequence they rise by 3 at every step.
All inputs are finite; a program needn't handle non-finite values.
Results may differ from a plain program's by a relative error of at most 0.015.
Values may be sent and summed in bfloat16 or wider, within the bound.
A program may use at most 192 MiB of HBM per device.

v0:
```python
import math

import jax
import jax.numpy as jnp
from jax import lax
from jax.sharding import PartitionSpec as P

HEAD_DIM = 64
SEQ_LEN = 1024


EPS = 1e-05
LOG_THETA = math.log(1000000.0)
MASKED = -1e30


def dot_plain(left, right):
    return jnp.dot(left, right, preferred_element_type=jnp.float32)


def dot_rows(left, right):
    return lax.dot_general(
        left, right, (((0,), (0,)), ((), ())), preferred_element_type=jnp.float32
    )


def dot_cols(left, right):
    return lax.dot_general(
        left, right, (((1,), (1,)), ((), ())), preferred_element_type=jnp.float32
    )


def normalize(values):
    inverse = lax.rsqrt(jnp.mean(values * values, axis=-1, keepdims=True) + EPS)
    return (values * inverse, inverse)


def norm_back(grad_unit, unit_values, inverse):
    return inverse * (
        grad_unit - unit_values * jnp.mean(grad_unit * unit_values, axis=-1, keepdims=True)
    )


def angles(positions):
    half_width = HEAD_DIM // 2
    frequency = jnp.exp(-LOG_THETA * 2.0 * jnp.arange(half_width, dtype=jnp.float32) / HEAD_DIM)
    rotation = positions.astype(jnp.float32)[:, None] * frequency[None, :]
    return (jnp.cos(rotation)[:, None, :], jnp.sin(rotation)[:, None, :])


def rotate(values, cosine, sine):
    half_width = HEAD_DIM // 2
    first_half = values[..., :half_width]
    second_half = values[..., half_width:]
    return jnp.concatenate(
        [first_half * cosine - second_half * sine, second_half * cosine + first_half * sine],
        axis=-1,
    )


def unrotate(grads, cosine, sine):
    half_width = HEAD_DIM // 2
    first_half = grads[..., :half_width]
    second_half = grads[..., half_width:]
    return jnp.concatenate(
        [first_half * cosine + second_half * sine, second_half * cosine - first_half * sine],
        axis=-1,
    )


def block_scores(query_block, key_seq, first_row):
    block_rows = query_block.shape[0]
    length = key_seq.shape[0]
    scores = jnp.einsum(
        "ikgd,jkd->kgij", query_block, key_seq, preferred_element_type=jnp.float32
    ) * HEAD_DIM ** (-0.5)
    allowed = (first_row + jnp.arange(block_rows))[:, None] >= jnp.arange(length)[None, :]
    return jnp.where(allowed, scores, MASKED)


def attention_forward(query_rot, key_rot, value_proj):
    length = query_rot.shape[1]
    block_rows = min(512, length)

    def one_sequence(sequence_items):
        query_seq, key_seq, value_seq = sequence_items
        pieces = []
        logsum_list = []
        for first_row in range(0, length, block_rows):
            query_block = query_seq[first_row : first_row + block_rows]
            scores = block_scores(query_block, key_seq, first_row)
            row_peak = jnp.max(scores, axis=-1, keepdims=True)
            row_total = jnp.sum(jnp.exp(scores - row_peak), axis=-1, keepdims=True)
            logsum = row_peak + jnp.log(row_total)
            softmax_prob = jnp.exp(scores - logsum)
            pieces.append(
                jnp.einsum(
                    "kgij,jkd->ikgd",
                    softmax_prob.astype(jnp.bfloat16),
                    value_seq,
                    preferred_element_type=jnp.float32,
                )
            )
            logsum_list.append(logsum)
        return (jnp.concatenate(pieces, axis=0), jnp.stack(logsum_list, axis=0))

    return lax.map(one_sequence, (query_rot, key_rot, value_proj))


def attention_backward(query_rot, key_rot, value_proj, grad_context, logsums):
    length = query_rot.shape[1]
    block_rows = min(512, length)
    score_scale = HEAD_DIM ** (-0.5)

    def one_sequence(sequence_items):
        query_seq, key_seq, value_seq, grad_seq, logsum_seq = sequence_items
        query_pieces = []
        key_total = jnp.zeros(key_seq.shape, jnp.float32)
        value_total = jnp.zeros(value_seq.shape, jnp.float32)
        for block_index, first_row in enumerate(range(0, length, block_rows)):
            query_block = query_seq[first_row : first_row + block_rows]
            grad_block = grad_seq[first_row : first_row + block_rows]
            scores = block_scores(query_block, key_seq, first_row)
            softmax_prob = jnp.exp(scores - logsum_seq[block_index])
            grad_prob = jnp.einsum(
                "ikgd,jkd->kgij", grad_block, value_seq, preferred_element_type=jnp.float32
            )
            row_inner = jnp.sum(softmax_prob * grad_prob, axis=-1, keepdims=True)
            grad_score = (softmax_prob * (grad_prob - row_inner)).astype(jnp.bfloat16)
            query_pieces.append(
                jnp.einsum(
                    "kgij,jkd->ikgd", grad_score, key_seq, preferred_element_type=jnp.float32
                )
                * score_scale
            )
            key_total = (
                key_total
                + jnp.einsum(
                    "kgij,ikgd->jkd", grad_score, query_block, preferred_element_type=jnp.float32
                )
                * score_scale
            )
            value_total = value_total + jnp.einsum(
                "kgij,ikgd->jkd",
                softmax_prob.astype(jnp.bfloat16),
                grad_block,
                preferred_element_type=jnp.float32,
            )
        return (jnp.concatenate(query_pieces, axis=0), key_total, value_total)

    return lax.map(one_sequence, (query_rot, key_rot, value_proj, grad_context, logsums))


def on_device(
    tokens,
    positions,
    first_gain,
    query_weight,
    key_weight,
    value_weight,
    query_gain,
    key_gain,
    out_weight,
    second_gain,
    gate_weight,
    up_weight,
    down_weight,
    cotangent,
):
    local_rows = tokens.shape[0]
    group_rows = positions.shape[0]
    sequences = group_rows // SEQ_LEN
    heads_here = query_weight.shape[1] // HEAD_DIM
    pairs_here = key_weight.shape[1] // HEAD_DIM
    share = heads_here // pairs_here
    whole_query, whole_key, whole_value, whole_out, whole_gate, whole_up, whole_down = (
        lax.all_gather(query_weight, "fsdp", axis=0, tiled=True),
        lax.all_gather(key_weight, "fsdp", axis=0, tiled=True),
        lax.all_gather(value_weight, "fsdp", axis=0, tiled=True),
        lax.all_gather(out_weight, "fsdp", axis=1, tiled=True),
        lax.all_gather(gate_weight, "fsdp", axis=0, tiled=True),
        lax.all_gather(up_weight, "fsdp", axis=0, tiled=True),
        lax.all_gather(down_weight, "fsdp", axis=1, tiled=True),
    )
    inputs = tokens.astype(jnp.float32)
    unit_one, inverse_one = normalize(inputs)
    normed_one = lax.all_gather(
        (unit_one * first_gain).astype(jnp.bfloat16), "tp", axis=0, tiled=True
    )
    query_proj = dot_plain(normed_one, whole_query).reshape(group_rows, heads_here, HEAD_DIM)
    key_proj = dot_plain(normed_one, whole_key).reshape(group_rows, pairs_here, HEAD_DIM)
    value_proj = dot_plain(normed_one, whole_value).astype(jnp.bfloat16)
    query_unit, query_inverse = normalize(query_proj)
    key_unit, key_inverse = normalize(key_proj)
    cosine, sine = angles(positions)
    query_rot = rotate(query_unit * query_gain, cosine, sine).astype(jnp.bfloat16)
    key_rot = rotate(key_unit * key_gain, cosine, sine).astype(jnp.bfloat16)
    shaped_query = query_rot.reshape(sequences, SEQ_LEN, pairs_here, share, HEAD_DIM)
    shaped_key = key_rot.reshape(sequences, SEQ_LEN, pairs_here, HEAD_DIM)
    shaped_value = value_proj.reshape(sequences, SEQ_LEN, pairs_here, HEAD_DIM)
    context, logsums = attention_forward(shaped_query, shaped_key, shaped_value)
    context = context.reshape(group_rows, heads_here * HEAD_DIM).astype(jnp.bfloat16)
    hidden = inputs + lax.psum_scatter(
        dot_plain(
            lax.slice_in_dim(context, 0, lax.axis_size("tp") * local_rows, axis=0), whole_out
        ),
        "tp",
        scatter_dimension=0,
        tiled=True,
    )
    unit_two, inverse_two = normalize(hidden)
    normed_two = lax.all_gather(
        (unit_two * second_gain).astype(jnp.bfloat16), "tp", axis=0, tiled=True
    )
    gate_value = dot_plain(normed_two, whole_gate)
    up_value = dot_plain(normed_two, whole_up)
    sigmoid_gate = jax.nn.sigmoid(gate_value)
    active = gate_value * sigmoid_gate
    mixed_units = (active * up_value).astype(jnp.bfloat16)
    result = hidden + lax.psum_scatter(
        dot_plain(
            lax.slice_in_dim(mixed_units, 0, local_rows * lax.axis_size("tp"), axis=0), whole_down
        ).astype(jnp.bfloat16),
        "tp",
        scatter_dimension=0,
        tiled=True,
    ).astype(jnp.float32)
    output = result.astype(jnp.bfloat16)
    back_query, back_key, back_value, back_out, back_gate, back_up, back_down = (
        lax.all_gather(query_weight, "fsdp", axis=0, tiled=True),
        lax.all_gather(key_weight, "fsdp", axis=0, tiled=True),
        lax.all_gather(value_weight, "fsdp", axis=0, tiled=True),
        lax.all_gather(out_weight, "fsdp", axis=1, tiled=True),
        lax.all_gather(gate_weight, "fsdp", axis=0, tiled=True),
        lax.all_gather(up_weight, "fsdp", axis=0, tiled=True),
        lax.all_gather(down_weight, "fsdp", axis=1, tiled=True),
    )
    grad_result = lax.all_gather(cotangent, "tp", axis=0, tiled=True)
    grad_down_w = dot_rows(mixed_units, grad_result)
    grad_mixed = dot_cols(grad_result, back_down)
    grad_gate = (
        grad_mixed * up_value * sigmoid_gate * (1.0 + gate_value * (1.0 - sigmoid_gate))
    ).astype(jnp.bfloat16)
    grad_up = (grad_mixed * active).astype(jnp.bfloat16)
    grad_gate_w = dot_rows(normed_two, grad_gate)
    grad_up_w = dot_rows(normed_two, grad_up)
    gate_rows = lax.slice_in_dim(grad_gate, 0, lax.axis_size("tp") * local_rows, axis=0)
    up_rows = lax.slice_in_dim(grad_up, 0, lax.axis_size("tp") * local_rows, axis=0)
    grad_normed_two = lax.psum_scatter(
        dot_cols(gate_rows, back_gate) + dot_cols(up_rows, back_up),
        "tp",
        scatter_dimension=0,
        tiled=True,
    )
    gain_two = jnp.sum(grad_normed_two * unit_two, axis=0)
    grad_hidden = cotangent.astype(jnp.float32) + norm_back(
        grad_normed_two * second_gain, unit_two, inverse_two
    )
    grad_hidden_all = lax.all_gather(grad_hidden.astype(jnp.bfloat16), "tp", axis=0, tiled=True)
    grad_out_w = dot_rows(context, grad_hidden_all)
    grad_context = dot_cols(grad_hidden_all, back_out).astype(jnp.bfloat16)
    grad_context = grad_context.reshape(sequences, SEQ_LEN, pairs_here, share, HEAD_DIM)
    grad_query_rot, grad_key_rot, grad_value_sum = attention_backward(
        shaped_query, shaped_key, shaped_value, grad_context, logsums
    )
    grad_query_normed = unrotate(
        grad_query_rot.reshape(group_rows, heads_here, HEAD_DIM), cosine, sine
    )
    grad_key_normed = unrotate(grad_key_rot.reshape(group_rows, pairs_here, HEAD_DIM), cosine, sine)
    gain_query = jnp.sum(grad_query_normed * query_unit, axis=(0, 1))
    gain_key = jnp.sum(grad_key_normed * key_unit, axis=(0, 1))
    grad_query = norm_back(grad_query_normed * query_gain, query_unit, query_inverse).astype(
        jnp.bfloat16
    )
    grad_query = grad_query.reshape(group_rows, heads_here * HEAD_DIM)
    grad_key = norm_back(grad_key_normed * key_gain, key_unit, key_inverse).astype(jnp.bfloat16)
    grad_key = grad_key.reshape(group_rows, pairs_here * HEAD_DIM)
    grad_value = grad_value_sum.astype(jnp.bfloat16).reshape(group_rows, pairs_here * HEAD_DIM)
    grad_query_w = dot_rows(normed_one, grad_query)
    grad_key_w = dot_rows(normed_one, grad_key)
    grad_value_w = dot_rows(normed_one, grad_value)
    value_rows = lax.slice_in_dim(grad_value, 0, local_rows * lax.axis_size("tp"), axis=0)
    grad_normed_one = lax.psum_scatter(
        (
            dot_cols(grad_query, back_query)
            + dot_cols(grad_key, back_key)
            + dot_cols(value_rows, back_value)
        ).astype(jnp.bfloat16),
        "tp",
        scatter_dimension=0,
        tiled=True,
    ).astype(jnp.float32)
    gain_one = jnp.sum(grad_normed_one * unit_one, axis=0)
    grad_tokens = grad_hidden + norm_back(grad_normed_one * first_gain, unit_one, inverse_one)
    weight_grads = (
        lax.psum_scatter(grad_query_w, "fsdp", scatter_dimension=0, tiled=True),
        lax.psum_scatter(grad_key_w, "fsdp", scatter_dimension=0, tiled=True),
        lax.psum_scatter(grad_value_w, "fsdp", scatter_dimension=0, tiled=True),
        lax.psum_scatter(grad_out_w, "fsdp", scatter_dimension=1, tiled=True),
        lax.psum_scatter(grad_gate_w, "fsdp", scatter_dimension=0, tiled=True),
        lax.psum_scatter(grad_up_w, "fsdp", scatter_dimension=0, tiled=True),
        lax.psum_scatter(grad_down_w, "fsdp", scatter_dimension=1, tiled=True),
    )
    gain_grads = lax.psum((gain_one, gain_query, gain_key, gain_two), ("fsdp", "tp"))
    return (
        output,
        grad_tokens,
        gain_grads[0],
        weight_grads[0],
        weight_grads[1],
        weight_grads[2],
        gain_grads[1],
        gain_grads[2],
        weight_grads[3],
        gain_grads[3],
        weight_grads[4],
        weight_grads[5],
        weight_grads[6],
    )


def solution(mesh):
    return jax.shard_map(
        on_device,
        mesh=mesh,
        in_specs=(
            P(("fsdp", "tp"), None),
            P("fsdp"),
            P(),
            P("fsdp", "tp"),
            P("fsdp", "tp"),
            P("fsdp", "tp"),
            P(),
            P(),
            P("tp", "fsdp"),
            P(),
            P("fsdp", "tp"),
            P("fsdp", "tp"),
            P("tp", "fsdp"),
            P(("fsdp", "tp"), None),
        ),
        out_specs=(
            P(("fsdp", "tp"), None),
            P(("fsdp", "tp"), None),
            P(),
            P("fsdp", "tp"),
            P("fsdp", "tp"),
            P("fsdp", "tp"),
            P(),
            P(),
            P("tp", "fsdp"),
            P(),
            P("fsdp", "tp"),
            P("fsdp", "tp"),
            P("tp", "fsdp"),
        ),
        check_vma=False,
    )
```

profile of v0, /device:TPU:0, one launch (start us, length us, event | category | flops | bytes accessed | tf_op | source)
XLA Modules:
  0.0 1453.8 jit_solution(977338290657508278)
XLA Ops:
  12.3 32.7 %all_gather.42 = bf16[1024,128]{1,0:T(8,128)(2,1)S(1)} all-gather(bf16[128,128]{1,0:T(8,128)(2,1)S(1)} %copy-done.45), channel_id=1, replica_groups=mesh['fsdp'=8,'tp'=4] {'fsdp'}, dimensions={0}, use_global_device_ids=true | all-gather | bytes 294912 | tf_op jit(solution)/shard_map/all_gather | solution.py:178
  45.0 30.8 %all_gather.41 = bf16[1024,128]{1,0:T(8,128)(2,1)S(1)} all-gather(bf16[128,128]{1,0:T(8,128)(2,1)S(1)} %copy-done.46), channel_id=1, replica_groups=mesh['fsdp'=8,'tp'=4] {'fsdp'}, dimensions={0}, use_global_device_ids=true | all-gather | bytes 294912 | tf_op jit(solution)/shard_map/all_gather | solution.py:179
  75.8 31.6 %all_gather.43 = bf16[1024,256]{1,0:T(8,128)(2,1)S(1)} all-gather(bf16[128,256]{1,0:T(8,128)(2,1)S(1)} %copy-done.40), channel_id=1, replica_groups=mesh['fsdp'=8,'tp'=4] {'fsdp'}, dimensions={0}, use_global_device_ids=true | all-gather | bytes 589824 | tf_op jit(solution)/shard_map/all_gather | solution.py:177
  107.4 28.1 %all_gather.44 = bf16[256,1024]{1,0:T(8,128)(2,1)} all-gather(bf16[256,128]{1,0:T(8,128)(2,1)S(1)} %copy-done.41), channel_id=1, replica_groups=mesh['fsdp'=8,'tp'=4] {'fsdp'}, dimensions={1}, use_global_device_ids=true | all-gather | bytes 589824 | tf_op jit(solution)/shard_map/all_gather | solution.py:180
  136.5 4.4 convolution_convert_fusion.2
  160.6 34.0 %while.26 = (s32[]{:T(128)}, bf16[2,1024,2,2,64]{1,4,3,2,0:T(8,128)(2,1)}, f32[2,2,2,2,512,1]{4,3,2,1,5,0:T(2,128)S(1)}, bf16[2,1024,2,64]{1,3,2,0:T(8,128)(2,1)...) while((s32[]{:T(128)}, ...), condition=%wide.region_8.9_spmd, body=%wide.region_3.8_spmd.sunk | while | flops 1121976832 | bytes 66214584 | solution.py:107
  198.3 4.6 fusion.115
  203.6 70.5 %reduce-scatter.12.cloned.1.call-done = f32[512,1024]{1,0:T(8,128)} async-done(((f32[2048,1024]{1,0:T(8,128)}), f32[512,1024]{1,0:T(8,128)}) %reduce-scatter.12.cloned.1.call-update) | async-done | bytes 2097168 | tf_op jit(solution)/shard_map/reduce_scatter | solution.py:203
  280.7 32.2 %all-gather.10.cloned.1.call-done = bf16[2048,1024]{1,0:T(8,128)(2,1)} async-done(((bf16[512,1024]{1,0:T(8,128)(2,1)}), bf16[2048,1024]{1,0:T(8,128)(2,1)}) %all-gather.10.cloned.1.call-update) | async-done | bytes 4194320 | tf_op jit(solution)/shard_map/all_gather | solution.py:212
  313.0 10.6 fusion.117
  323.5 43.5 %all-gather.12.cloned.1.call-done = bf16[1024,1152]{1,0:T(8,128)(2,1)} async-done(((bf16[128,1152]{1,0:T(8,128)(2,1)}), bf16[1024,1152]{1,0:T(8,128)(2,1)}) %all-gather.12.cloned.1.call-update) | async-done | bytes 2359312 | tf_op jit(solution)/shard_map/all_gather | solution.py:181
  367.0 10.2 fusion.116
  377.3 44.3 %all-gather.16.cloned.1.call-done = bf16[1152,1024]{1,0:T(8,128)(2,1)} async-done(((bf16[1152,128]{1,0:T(8,128)(2,1)}), bf16[1152,1024]{1,0:T(8,128)(2,1)}) %all-gather.16.cloned.1.call-update) | async-done | bytes 2359312 | tf_op jit(solution)/shard_map/all_gather | solution.py:183
  421.5 34.2 %all-gather.18.cloned.1.call-done = bf16[2048,1024]{1,0:T(8,128)(2,1)} async-done(((bf16[512,1024]{1,0:T(8,128)(2,1)}), bf16[2048,1024]{1,0:T(8,128)(2,1)}) %all-gather.18.cloned.1.call-update) | async-done | bytes 4194320 | tf_op jit(solution)/shard_map/all_gather | solution.py:238
  455.7 17.7 %multiply_convert_fusion = (bf16[2048,1152]{1,0:T(8,128)(2,1)}, bf16[2048,1152]{1,0:T(8,128)(2,1)}, bf16[2048,1152]{1,0:T(8,128)(2,1)}) fusion(f32[2048,1152]{1,0:T(8,128)} %fusion.116, f32[2048,1152]{1,0:T(8,128)} %fusion.117, bf16[2048,1024]{1,0:T(8,128)(2,1)} %all-gather.18.cloned.1.call-done, bf16[1152,1024]{1,0:T(8,128)(2,1)} %all-gather.16.cloned.1.call-done), kind=kOutput, calls=%fused_computation.119 | convolution fusion | flops 4867227648 | bytes 39583744 | tf_op jit(solution)/shard_map/dot_general | solution.py:28
  473.4 8.4 fusion.118
  481.8 8.5 convolution_add_fusion
  490.4 71.8 %reduce-scatter.16.cloned.1.call-done = f32[512,1024]{1,0:T(8,128)} async-done(((f32[2048,1024]{1,0:T(8,128)}), f32[512,1024]{1,0:T(8,128)}) %reduce-scatter.16.cloned.1.call-update) | async-done | bytes 2097168 | tf_op jit(solution)/shard_map/reduce_scatter | solution.py:249
  570.4 33.1 %all-gather.20.cloned.1.call-done = bf16[2048,1024]{1,0:T(8,128)(2,1)} async-done(((bf16[512,1024]{1,0:T(8,128)(2,1)}), bf16[2048,1024]{1,0:T(8,128)(2,1)}) %all-gather.20.cloned.1.call-update) | async-done | bytes 4194320 | tf_op jit(solution)/shard_map/all_gather | solution.py:259
  608.8 5.9 copy.79
  614.7 154.7 %while.27 = (s32[]{:T(128)}, f32[2,1024,2,2,64]{1,0,4,3,2:T(2,128)}, f32[2,1024,2,64]{1,0,3,2:T(2,128)}, bf16[2,1024,2,64]{1,3,2,0:T(8,128)(2,1)}, bf16[2,1024,2...) while((s32[]{:T(128)}, ...), condition=%wide.region_17.18_spmd, body=%wide.region_14.17_spmd.sunk | while | flops 2749231616 | bytes 234482448 | solution.py:151
  625.9 5.9 fusion.221
  631.8 5.9 fusion.223
  637.7 15.0 %fusion.224 = (bf16[2,2,512,1024]{2,3,1,0:T(8,128)(2,1)}, bf16[2,2,512,1024]{2,3,1,0:T(8,128)(2,1)S(1)}) fusion(f32[2,1024,512,2]{2,1,3,0:T(8,128)} %get-tuple-element.333, f32[2,1024,512,2]{2,1,3,0:T(8,128)} %copy-done, f32[2,2,512]{2,1,0:T(2,128)S(1)} %get-tuple-element.334, f32[2,2,512]{2,1,0:T(2,128)S(1)} %get-tuple-element.332, ...), kind=kLoop, calls=%fused_computation.47.clone.1 | loop fusion | flops 25165824 | bytes 43024384 | tf_op jit(solution)/shard_map/while/body/eval_jaxpr/convert_element_type | solution.py:129
  663.1 10.0 dynamic_update_slice.30
  673.1 18.8 %dynamic_update_slice.29 = f32[2,1024,2,2,64]{1,0,4,3,2:T(2,128)} dynamic-update-slice(f32[2,1024,2,2,64]{1,0,4,3,2:T(2,128)} %get-tuple-element.381, f32[1,1024,2,2,64]{1,0,4,3,2:T(1,128)S(1)} %copy.125, s32[]{:T(128)S(6)} %copy.145, s32[]{:T(128)} %constant.73.clone.1..sunk.1, s32[]{:T(128)} %constant.73.clone.1..sunk.1, s32[]{:T(128)} %constant.73.clone.1..sunk.1, s32[]{:T(128)} %constant.73.clone.1..sunk.1) | dynamic-update-slice | bytes 2097156 | tf_op jit(solution)/shard_map/while/body/jit(dynamic_update_index_in_dim)/dynamic_update_slice | solution.py:107
  703.1 5.9 fusion.221
  709.0 5.9 fusion.223
  714.8 15.0 %fusion.224 = (bf16[2,2,512,1024]{2,3,1,0:T(8,128)(2,1)}, bf16[2,2,512,1024]{2,3,1,0:T(8,128)(2,1)S(1)}) fusion(f32[2,1024,512,2]{2,1,3,0:T(8,128)} %get-tuple-element.333, f32[2,1024,512,2]{2,1,3,0:T(8,128)} %copy-done, f32[2,2,512]{2,1,0:T(2,128)S(1)} %get-tuple-element.334, f32[2,2,512]{2,1,0:T(2,128)S(1)} %get-tuple-element.332, ...), kind=kLoop, calls=%fused_computation.47.clone.1 | loop fusion | flops 25165824 | bytes 43024384 | tf_op jit(solution)/shard_map/while/body/eval_jaxpr/convert_element_type | solution.py:129
  740.3 10.0 dynamic_update_slice.30
  750.3 18.8 %dynamic_update_slice.29 = f32[2,1024,2,2,64]{1,0,4,3,2:T(2,128)} dynamic-update-slice(f32[2,1024,2,2,64]{1,0,4,3,2:T(2,128)} %get-tuple-element.381, f32[1,1024,2,2,64]{1,0,4,3,2:T(1,128)S(1)} %copy.125, s32[]{:T(128)S(6)} %copy.145, s32[]{:T(128)} %constant.73.clone.1..sunk.1, s32[]{:T(128)} %constant.73.clone.1..sunk.1, s32[]{:T(128)} %constant.73.clone.1..sunk.1, s32[]{:T(128)} %constant.73.clone.1..sunk.1) | dynamic-update-slice | bytes 2097156 | tf_op jit(solution)/shard_map/while/body/jit(dynamic_update_index_in_dim)/dynamic_update_slice | solution.py:107
  791.1 9.5 convolution_convert_fusion
  800.7 10.2 fusion.127
  811.0 10.3 fusion.126
  821.4 10.3 fusion.125
  831.8 4.3 fusion.123
  836.2 4.3 fusion.122
  840.6 4.4 fusion.124
  845.4 6.2 fusion.121
  853.9 40.2 %all-reduce = (f32[1024]{0:T(1024)}, f32[64]{0:T(128)}, f32[64]{0:T(128)}, f32[1024]{0:T(1024)}) all-reduce(f32[1024]{0:T(1024)S(1)} %get-tuple-element.147, f32[64]{0:T(128)S(1)} %reduce_sum.169, f32[64]{0:T(128)S(1)} %reduce_sum.172, f32[1024]{0:T(1024)S(1)} %copy-done.51), channel_id=1, replica_groups=mesh['fsdp'=8,'tp'=4] {'fsdp','tp'}, use_global_device_ids=true, to_apply=%region_23.24 | all-reduce | flops 2176 | bytes 17408 | tf_op jit(solution)/shard_map/psum | solution.py:304
  894.2 4.5 fusion.103
  898.6 84.5 %reduce-scatter.32.cloned.1.call-done = f32[1152,128]{1,0:T(8,128)} async-done(((f32[1152,1024]{1,0:T(8,128)}), f32[1152,128]{1,0:T(8,128)}) %reduce-scatter.32.cloned.1.call-update) | async-done | bytes 589840 | tf_op jit(solution)/shard_map/reduce_scatter | solution.py:302
  983.1 99.1 %reduce-scatter.30.cloned.1.call-done = f32[128,1152]{1,0:T(8,128)} async-done(((f32[1024,1152]{1,0:T(8,128)}), f32[128,1152]{1,0:T(8,128)}) %reduce-scatter.30.cloned.1.call-update) | async-done | bytes 589840 | tf_op jit(solution)/shard_map/reduce_scatter | solution.py:301
  1082.3 99.0 %reduce-scatter.28.cloned.1.call-done = f32[128,1152]{1,0:T(8,128)} async-done(((f32[1024,1152]{1,0:T(8,128)}), f32[128,1152]{1,0:T(8,128)}) %reduce-scatter.28.cloned.1.call-update) | async-done | bytes 589840 | tf_op jit(solution)/shard_map/reduce_scatter | solution.py:300
  1181.2 65.6 %reduce-scatter.24.cloned.1.call-done = f32[128,128]{1,0:T(8,128)} async-done(((f32[1024,128]{1,0:T(8,128)}), f32[128,128]{1,0:T(8,128)}) %reduce-scatter.24.cloned.1.call-update) | async-done | bytes 65552 | tf_op jit(solution)/shard_map/reduce_scatter | solution.py:298
  1246.9 65.2 %reduce-scatter.22.cloned.1.call-done = f32[128,128]{1,0:T(8,128)} async-done(((f32[1024,128]{1,0:T(8,128)}), f32[128,128]{1,0:T(8,128)}) %reduce-scatter.22.cloned.1.call-update) | async-done | bytes 65552 | tf_op jit(solution)/shard_map/reduce_scatter | solution.py:297
  1312.1 67.2 %reduce-scatter.26.cloned.1.call-done = f32[256,128]{1,0:T(8,128)} async-done(((f32[256,1024]{1,0:T(8,128)}), f32[256,128]{1,0:T(8,128)}) %reduce-scatter.26.cloned.1.call-update) | async-done | bytes 131088 | tf_op jit(solution)/shard_map/reduce_scatter | solution.py:299
  1379.3 67.0 %reduce-scatter.20.cloned.1.call-done = f32[128,256]{1,0:T(8,128)} async-done(((f32[1024,256]{1,0:T(8,128)}), f32[128,256]{1,0:T(8,128)}) %reduce-scatter.20.cloned.1.call-update) | async-done | bytes 131088 | tf_op jit(solution)/shard_map/reduce_scatter | solution.py:296
  (298 shorter events, 150.2 us)
Async XLA Ops:
  8.0 36.9 %copy-start.46 = (bf16[128,128]{1,0:T(8,128)(2,1)S(1)}, bf16[128,128]{1,0:T(8,128)(2,1)}, u32[]{:S(2)}) copy-start(bf16[128,128]{1,0:T(8,128)(2,1)} %param.23) | copy-start | bytes 98308
  8.0 67.7 %copy-start.40 = (bf16[128,256]{1,0:T(8,128)(2,1)S(1)}, bf16[128,256]{1,0:T(8,128)(2,1)}, u32[]{:S(2)}) copy-start(bf16[128,256]{1,0:T(8,128)(2,1)} %param.21) | copy-start | bytes 196612
  8.1 99.3 %copy-start.41 = (bf16[256,128]{1,0:T(8,128)(2,1)S(1)}, bf16[256,128]{1,0:T(8,128)(2,1)}, u32[]{:S(2)}) copy-start(bf16[256,128]{1,0:T(8,128)(2,1)} %param.26) | copy-start | bytes 196612
  8.1 128.4 %all-gather.8.cloned.1.call-start = ((), (), s32[]{:S(2)}) async-start(), calls=%async_computation.11 | async-start | bytes 5242880 | tf_op jit(solution)/shard_map/all_gather | solution.py:187
  12.2 261.8 %reduce-scatter.12.cloned.1.call-start = ((), (), s32[]{:S(2)}) async-start(), calls=%async_computation.12 | async-start | bytes 10485760 | tf_op jit(solution)/shard_map/reduce_scatter | solution.py:203
  45.0 100.3 %copy-start.25 = (bf16[1024,128]{1,0:T(8,128)(2,1)}, bf16[1024,128]{1,0:T(8,128)(2,1)S(1)}, u32[]{:S(2)}) copy-start(bf16[1024,128]{1,0:T(8,128)(2,1)S(1)} %all_gather.42) | copy-start | bytes 786436
  75.8 67.6 %copy-start.32 = (bf16[1024,128]{1,0:T(8,128)(2,1)}, bf16[1024,128]{1,0:T(8,128)(2,1)S(1)}, u32[]{:S(2)}) copy-start(bf16[1024,128]{1,0:T(8,128)(2,1)S(1)} %all_gather.41) | copy-start | bytes 786436
  107.4 44.2 %copy-start.27 = (bf16[1024,256]{1,0:T(8,128)(2,1)}, bf16[1024,256]{1,0:T(8,128)(2,1)S(1)}, u32[]{:S(2)}) copy-start(bf16[1024,256]{1,0:T(8,128)(2,1)S(1)} %all_gather.43) | copy-start | bytes 1572868
  136.5 20.4 %copy-start.14 = (f32[2048,32]{0,1:T(8,128)}, f32[2048,32]{0,1:T(8,128)S(1)}, u32[]{:S(2)}) copy-start(f32[2048,32]{0,1:T(8,128)S(1)} %get-tuple-element.218) | copy-start | bytes 786436
  136.5 20.4 %copy-start.16 = (f32[2048,32]{0,1:T(8,128)}, f32[2048,32]{0,1:T(8,128)S(1)}, u32[]{:S(2)}) copy-start(f32[2048,32]{0,1:T(8,128)S(1)} %get-tuple-element.219) | copy-start | bytes 786436
  140.9 9.1 copy-start.57
  202.9 71.1 %copy-start.5 = (bf16[512,1024]{1,0:T(8,128)(2,1)S(1)}, bf16[512,1024]{1,0:T(8,128)(2,1)}, u32[]{:S(2)}) copy-start(bf16[512,1024]{1,0:T(8,128)(2,1)} %param.18) | copy-start | bytes 3145732
  202.9 74.4 %copy-start.38 = (f32[1024]{0:T(1024)S(1)}, f32[1024]{0:T(1024)}, u32[]{:S(2)}) copy-start(f32[1024]{0:T(1024)} %param.27) | copy-start | bytes 12292
  202.9 77.8 %all-gather.14.cloned.1.call-start = ((), (), s32[]{:S(2)}) async-start(), calls=%async_computation.15 | async-start | bytes 2654208 | tf_op jit(solution)/shard_map/all_gather | solution.py:182
  203.5 109.4 %all-gather.10.cloned.1.call-start = ((), (), s32[]{:S(2)}) async-start(), calls=%async_computation.13 | async-start | bytes 5242880 | tf_op jit(solution)/shard_map/all_gather | solution.py:212
  276.0 289.8 %copy-start.42 = (f32[512]{0:T(512)}, f32[512]{0:T(512)S(1)}, u32[]{:S(2)}) copy-start(f32[512]{0:T(512)S(1)} %add_rsqrt_fusion.2) | copy-start | bytes 6148
  278.6 88.5 %all-gather.12.cloned.1.call-start = ((), (), s32[]{:S(2)}) async-start(), calls=%async_computation.14 | async-start | bytes 2654208 | tf_op jit(solution)/shard_map/all_gather | solution.py:181
  279.1 142.4 %all-gather.16.cloned.1.call-start = ((), (), s32[]{:S(2)}) async-start(), calls=%async_computation.16 | async-start | bytes 2654208 | tf_op jit(solution)/shard_map/all_gather | solution.py:183
  279.9 175.8 %all-gather.18.cloned.1.call-start = ((), (), s32[]{:S(2)}) async-start(), calls=%async_computation.18 | async-start | bytes 5242880 | tf_op jit(solution)/shard_map/all_gather | solution.py:238
  280.6 281.6 %reduce-scatter.16.cloned.1.call-start = ((), (), s32[]{:S(2)}) async-start(), calls=%async_computation.19 | async-start | bytes 10485760 | tf_op jit(solution)/shard_map/reduce_scatter | solution.py:249
  473.4 8.4 copy-start.61
  473.4 8.4 copy-start.62
  490.4 75.4 %copy-start.13 = (bf16[512,1024]{1,0:T(8,128)(2,1)S(1)}, bf16[512,1024]{1,0:T(8,128)(2,1)}, u32[]{:S(2)}) copy-start(bf16[512,1024]{1,0:T(8,128)(2,1)} %param.31) | copy-start | bytes 3145732
  490.4 113.1 %all-gather.20.cloned.1.call-start = ((), (), s32[]{:S(2)}) async-start(), calls=%async_computation.20 | async-start | bytes 5242880 | tf_op jit(solution)/shard_map/all_gather | solution.py:259
  565.8 41.2 %copy-start.49 = (f32[512]{0:T(512)}, f32[512]{0:T(512)S(1)}, u32[]{:S(2)}) copy-start(f32[512]{0:T(512)S(1)} %broadcast_multiply_fusion.3) | copy-start | bytes 6148
  569.1 282.8 %reduce-scatter.18.cloned.1.call-start = ((), (), s32[]{:S(2)}) async-start(), calls=%async_computation.21 | async-start | bytes 5242880 | tf_op jit(solution)/shard_map/reduce_scatter | solution.py:283
  617.6 14.2 copy-start.1
  694.8 14.2 copy-start.1
  729.9 5.5 copy-start.2
  775.6 6.2 copy-start.8
  775.6 6.2 copy-start.35
  775.6 6.2 copy-start.55
  791.1 103.1 %reduce-scatter.14.cloned.1.call-start = ((), (), s32[]{:S(2)}) async-start(), calls=%async_computation.17 | async-start | bytes 5242880 | tf_op jit(solution)/shard_map/reduce_scatter | solution.py:220
  800.6 182.5 %reduce-scatter.32.cloned.1.call-start = ((), (), s32[]{:S(2)}) async-start(), calls=%async_computation.28 | async-start | bytes 5308416 | tf_op jit(solution)/shard_map/reduce_scatter | solution.py:302
  810.9 271.4 %reduce-scatter.30.cloned.1.call-start = ((), (), s32[]{:S(2)}) async-start(), calls=%async_computation.27 | async-start | bytes 5308416 | tf_op jit(solution)/shard_map/reduce_scatter | solution.py:301
  821.3 359.9 %reduce-scatter.28.cloned.1.call-start = ((), (), s32[]{:S(2)}) async-start(), calls=%async_computation.26 | async-start | bytes 5308416 | tf_op jit(solution)/shard_map/reduce_scatter | solution.py:300
  831.7 415.2 %reduce-scatter.24.cloned.1.call-start = ((), (), s32[]{:S(2)}) async-start(), calls=%async_computation.24 | async-start | bytes 589824 | tf_op jit(solution)/shard_map/reduce_scatter | solution.py:298
  836.1 476.0 %reduce-scatter.22.cloned.1.call-start = ((), (), s32[]{:S(2)}) async-start(), calls=%async_computation.23 | async-start | bytes 589824 | tf_op jit(solution)/shard_map/reduce_scatter | solution.py:297
  840.5 538.7 %reduce-scatter.26.cloned.1.call-start = ((), (), s32[]{:S(2)}) async-start(), calls=%async_computation.25 | async-start | bytes 1179648 | tf_op jit(solution)/shard_map/reduce_scatter | solution.py:299
  845.0 6.8 copy-start.6
  845.1 6.8 copy-start.44
  845.1 6.8 copy-start.48
  845.1 8.9 copy-start.51
  845.1 49.0 %copy-start.4 = (f32[512,1024]{1,0:T(8,128)S(1)}, f32[512,1024]{1,0:T(8,128)}, u32[]{:S(2)}) copy-start(f32[512,1024]{1,0:T(8,128)} %copy-done.3) | copy-start | bytes 6291460
  845.1 49.0 %copy-start.39 = (f32[1024]{0:T(1024)S(1)}, f32[1024]{0:T(1024)}, u32[]{:S(2)}) copy-start(f32[1024]{0:T(1024)} %param.27) | copy-start | bytes 12292
  845.1 49.0 %copy-start.43 = (f32[512]{0:T(512)S(1)}, f32[512]{0:T(512)}, u32[]{:S(2)}) copy-start(f32[512]{0:T(512)} %copy-done.42) | copy-start | bytes 6148
  845.1 49.0 %copy-start.50 = (f32[512]{0:T(512)S(1)}, f32[512]{0:T(512)}, u32[]{:S(2)}) copy-start(f32[512]{0:T(512)} %copy-done.49) | copy-start | bytes 6148
  845.1 601.1 %reduce-scatter.20.cloned.1.call-start = ((), (), s32[]{:S(2)}) async-start(), calls=%async_computation.22 | async-start | bytes 1179648 | tf_op jit(solution)/shard_map/reduce_scatter | solution.py:296
  (39 other events, 108.7 us)
Sparse Core Ops, SparseCore 0:
  12.3 37.1 all-gather.7
  203.0 70.9 reduce-scatter.11
  490.5 71.6 reduce-scatter.15
Sparse Core Ops, SparseCore 1:
  205.6 50.9 all-gather.13
  278.6 34.3 all-gather.9
  315.2 51.7 all-gather.11
  369.3 52.2 all-gather.15
  423.2 32.5 all-gather.17
  569.1 34.3 all-gather.19
  791.1 44.4 reduce-scatter.17
  838.2 45.1 reduce-scatter.13
  887.4 95.6 reduce-scatter.31
  987.4 94.8 reduce-scatter.29
  1086.4 94.8 reduce-scatter.27
  1185.2 61.6 reduce-scatter.23
  1251.0 61.0 reduce-scatter.21
  1316.1 63.1 reduce-scatter.25
  1383.6 62.5 reduce-scatter.19
where the time goes:
time: 1470 us; the launch traced here: 1450 us
  waiting for transfers between devices  880 us (60%)
  matrix products  226 us (15%)
  blocking collectives  163 us (11%)
  local copies, waits for them, and re-layouts  96.4 us (7%)
  other arithmetic  69.7 us (5%)
  between operations  16.8 us (1%)
    reduce_scatter x1, waiting for transfers between devices, on_device(): lax.psum_scatter(grad_up_w, 'fsdp', scatter_dimension=0, tiled=True)  99.1 us
    reduce_scatter x1, waiting for transfers between devices, on_device(): lax.psum_scatter(grad_gate_w, 'fsdp', scatter_dimension=0, tiled=True)  99 us
    reduce_scatter x1, waiting for transfers between devices, on_device(): lax.psum_scatter(grad_down_w, 'fsdp', scatter_dimension=1, tiled=True)  84.5 us
    reduce_scatter x1, waiting for transfers between devices, on_device(): lax.psum_scatter(dot_cols(gate_rows, back_gate) + dot_cols(up_rows, back_...  71.8 us
    reduce_scatter x1, waiting for transfers between devices, on_device(): lax.psum_scatter(dot_plain(lax.slice_in_dim(context, 0, lax.axis_size('tp...  70.5 us
    reduce_scatter x1, waiting for transfers between devices, on_device(): lax.psum_scatter(grad_out_w, 'fsdp', scatter_dimension=1, tiled=True)  67.2 us
    reduce_scatter x1, waiting for transfers between devices, on_device(): lax.psum_scatter(grad_query_w, 'fsdp', scatter_dimension=0, tiled=True)  67 us
    reduce_scatter x1, waiting for transfers between devices, on_device(): lax.psum_scatter(grad_value_w, 'fsdp', scatter_dimension=0, tiled=True)  65.6 us
  transfers between devices with their start and end apart: 18, of which 14 were waited for; matrix products, arithmetic and copies ran while one was open for 6% of the time, Pallas kernels for 0%

commit v1 on v0

v1 whole, which is shorter than its diff:
```python
import functools
import math

import jax
import jax.numpy as jnp
from jax import lax
from jax.experimental import pallas as pl
from jax.experimental.pallas import tpu as pltpu
from jax.sharding import PartitionSpec as P

HEAD_DIM = 64
SEQ_LEN = 1024


EPS = 1e-05
LOG_THETA = math.log(1000000.0)
MASKED = -1e30


def dot_plain(left, right):
    return jnp.dot(left, right, preferred_element_type=jnp.float32)


def dot_rows(left, right):
    return lax.dot_general(
        left, right, (((0,), (0,)), ((), ())), preferred_element_type=jnp.float32
    )


def dot_cols(left, right):
    return lax.dot_general(
        left, right, (((1,), (1,)), ((), ())), preferred_element_type=jnp.float32
    )


def normalize(values):
    inverse = lax.rsqrt(jnp.mean(values * values, axis=-1, keepdims=True) + EPS)
    return (values * inverse, inverse)


def norm_back(grad_unit, unit_values, inverse):
    return inverse * (
        grad_unit - unit_values * jnp.mean(grad_unit * unit_values, axis=-1, keepdims=True)
    )


def angle_tables(positions):
    half_width = HEAD_DIM // 2
    frequency = jnp.exp(-LOG_THETA * 2.0 * jnp.arange(half_width, dtype=jnp.float32) / HEAD_DIM)
    rotation = positions.astype(jnp.float32)[None, :] * frequency[:, None]
    cosine, sine = jnp.cos(rotation), jnp.sin(rotation)
    cosine_table = jnp.concatenate([cosine, cosine, cosine, cosine], axis=0).T
    sine_table = jnp.concatenate([-sine, sine, -sine, sine], axis=0).T
    return (cosine_table, sine_table)


def widen(table, width):
    return jnp.concatenate([table] * (width // table.shape[1]), axis=1)


def swap_halves(values):
    width = values.shape[1]
    half_width = HEAD_DIM // 2
    lane = lax.broadcasted_iota(jnp.int32, values.shape, 1)
    ahead = pltpu.roll(values, width - half_width, 1)
    behind = pltpu.roll(values, half_width, 1)
    return jnp.where(lane % HEAD_DIM < half_width, ahead, behind)


def head_mean(values):
    width = values.shape[1]
    row_head = lax.broadcasted_iota(jnp.int32, (width, width), 0) // HEAD_DIM
    col_head = lax.broadcasted_iota(jnp.int32, (width, width), 1) // HEAD_DIM
    spread = jnp.where(row_head == col_head, 1.0 / HEAD_DIM, 0.0).astype(jnp.float32)
    return jnp.dot(
        values, spread, preferred_element_type=jnp.float32, precision=lax.Precision.HIGHEST
    )


def head_units(values):
    inverse = lax.rsqrt(head_mean(values * values) + EPS)
    return (values * inverse, inverse)


def masked_scores(key_rows, query_rows, first_row, block_rows):
    scores = dot_cols(key_rows, query_rows)
    key_index = lax.broadcasted_iota(jnp.int32, scores.shape, 0)
    row_index = first_row + lax.broadcasted_iota(jnp.int32, scores.shape, 1) % block_rows
    return jnp.where(key_index <= row_index, scores, MASKED)


def stacked_heads(ref, first_row, block_rows, pair, share):
    return jnp.concatenate(
        [
            ref[
                first_row : first_row + block_rows,
                (pair * share + member) * HEAD_DIM : (pair * share + member + 1) * HEAD_DIM,
            ]
            for member in range(share)
        ],
        axis=0,
    )


def forward_kernel(
    pairs, share, block_rows, proj_ref, cosine_ref, sine_ref, query_gain_ref, key_gain_ref,
    rot_ref, context_ref, logsum_ref,
):
    length = proj_ref.shape[0]
    query_width = pairs * share * HEAD_DIM
    key_width = pairs * HEAD_DIM
    cosine, sine = cosine_ref[...], sine_ref[...]
    query_unit, _ = head_units(proj_ref[:, :query_width])
    key_unit, _ = head_units(proj_ref[:, query_width : query_width + key_width])
    query_scaled = query_unit * query_gain_ref[...]
    key_scaled = key_unit * key_gain_ref[...]
    rot_ref[:, :query_width] = (
        query_scaled * widen(cosine, query_width)
        + swap_halves(query_scaled) * widen(sine, query_width)
    ).astype(jnp.bfloat16)
    rot_ref[:, query_width : query_width + key_width] = (
        key_scaled * widen(cosine, key_width) + swap_halves(key_scaled) * widen(sine, key_width)
    ).astype(jnp.bfloat16)
    rot_ref[:, query_width + key_width :] = proj_ref[:, query_width + key_width :].astype(
        jnp.bfloat16
    )
    for pair in range(pairs):
        key_lanes = slice(query_width + pair * HEAD_DIM, query_width + (pair + 1) * HEAD_DIM)
        value_lanes = slice(key_lanes.start + key_width, key_lanes.stop + key_width)
        for first_row in range(0, length, block_rows):
            last_row = first_row + block_rows
            query_rows = stacked_heads(rot_ref, first_row, block_rows, pair, share)
            query_rows = query_rows * jnp.asarray(HEAD_DIM ** (-0.5), jnp.bfloat16)
            scores = masked_scores(
                rot_ref[:last_row, key_lanes], query_rows, first_row, block_rows
            )
            weights = jnp.exp(scores)
            total = jnp.sum(weights, axis=0, keepdims=True)
            context = dot_rows(rot_ref[:last_row, value_lanes], weights.astype(jnp.bfloat16))
            context = (context / total).T.astype(jnp.bfloat16)
            logsum = jnp.log(total)
            for member in range(share):
                head = pair * share + member
                here = slice(member * block_rows, (member + 1) * block_rows)
                context_ref[
                    first_row:last_row, head * HEAD_DIM : (head + 1) * HEAD_DIM
                ] = context[here]
                logsum_ref[head : head + 1, first_row:last_row] = logsum[:, here]


def backward_kernel(
    pairs, share, block_rows, proj_ref, cosine_ref, sine_ref, query_gain_ref, key_gain_ref,
    rot_ref, logsum_ref, grad_context_ref,
    grad_proj_ref, gain_sum_ref, query_total, key_total, value_total,
):
    length = proj_ref.shape[0]
    query_width = pairs * share * HEAD_DIM
    key_width = pairs * HEAD_DIM
    scale = HEAD_DIM ** (-0.5)
    for pair in range(pairs):
        key_lanes = slice(query_width + pair * HEAD_DIM, query_width + (pair + 1) * HEAD_DIM)
        value_lanes = slice(key_lanes.start + key_width, key_lanes.stop + key_width)
        pair_lanes = slice(pair * HEAD_DIM, (pair + 1) * HEAD_DIM)
        for first_row in reversed(range(0, length, block_rows)):
            last_row = first_row + block_rows
            query_rows = stacked_heads(rot_ref, first_row, block_rows, pair, share)
            query_rows = query_rows * jnp.asarray(scale, jnp.bfloat16)
            grad_rows = stacked_heads(grad_context_ref, first_row, block_rows, pair, share)
            logsum = jnp.concatenate(
                [
                    logsum_ref[pair * share + member : pair * share + member + 1, first_row:last_row]
                    for member in range(share)
                ],
                axis=1,
            )
            key_rows = rot_ref[:last_row, key_lanes]
            scores = masked_scores(key_rows, query_rows, first_row, block_rows)
            prob = jnp.exp(scores - logsum)
            grad_prob = dot_cols(rot_ref[:last_row, value_lanes], grad_rows)
            inner = jnp.sum(prob * grad_prob, axis=0, keepdims=True)
            grad_score = (prob * (grad_prob - inner)).astype(jnp.bfloat16)
            grad_query = (dot_rows(key_rows, grad_score) * scale).T
            for member in range(share):
                head = pair * share + member
                query_total[
                    first_row:last_row, head * HEAD_DIM : (head + 1) * HEAD_DIM
                ] = grad_query[member * block_rows : (member + 1) * block_rows]
            grad_key = dot_plain(grad_score, query_rows)
            grad_value = dot_plain(prob.astype(jnp.bfloat16), grad_rows)
            if last_row == length:
                key_total[:, pair_lanes] = grad_key
                value_total[:, pair_lanes] = grad_value
            else:
                key_total[:last_row, pair_lanes] += grad_key
                value_total[:last_row, pair_lanes] += grad_value
    cosine, sine = cosine_ref[...], sine_ref[...]
    for lanes, total, gain_ref in (
        (slice(0, query_width), query_total, query_gain_ref),
        (slice(query_width, query_width + key_width), key_total, key_gain_ref),
    ):
        width = lanes.stop - lanes.start
        unit, inverse = head_units(proj_ref[:, lanes])
        grads = total[...]
        grad_normed = grads * widen(cosine, width) - swap_halves(grads) * widen(sine, width)
        gain_sum_ref[0:1, lanes] = jnp.sum(grad_normed * unit, axis=0, keepdims=True)
        scaled = grad_normed * gain_ref[...]
        grad_proj_ref[:, lanes] = (
            inverse * (scaled - unit * head_mean(scaled * unit))
        ).astype(jnp.bfloat16)
    grad_proj_ref[:, query_width + key_width :] = value_total[...].astype(jnp.bfloat16)


def row_spec(width):
    return pl.BlockSpec((SEQ_LEN, width), lambda sequence: (sequence, 0))


def whole_spec(width):
    return pl.BlockSpec((1, width), lambda sequence: (0, 0))


def attention_forward(proj, tables, gain_rows, pairs, share):
    rows, width = proj.shape
    query_width = pairs * share * HEAD_DIM
    key_width = pairs * HEAD_DIM
    sequences = rows // SEQ_LEN
    return pl.pallas_call(
        functools.partial(forward_kernel, pairs, share, min(256, SEQ_LEN)),
        grid=(sequences,),
        in_specs=[
            row_spec(width), row_spec(128), row_spec(128),
            whole_spec(query_width), whole_spec(key_width),
        ],
        out_specs=[
            row_spec(width),
            row_spec(query_width),
            pl.BlockSpec((8, SEQ_LEN), lambda sequence: (sequence, 0)),
        ],
        out_shape=[
            jax.ShapeDtypeStruct((rows, width), jnp.bfloat16),
            jax.ShapeDtypeStruct((rows, query_width), jnp.bfloat16),
            jax.ShapeDtypeStruct((sequences * 8, SEQ_LEN), jnp.float32),
        ],
        compiler_params=pltpu.CompilerParams(vmem_limit_bytes=48 * 1024 * 1024),
        cost_estimate=pl.CostEstimate(
            flops=4 * rows * SEQ_LEN * query_width,
            bytes_accessed=10 * rows * width,
            transcendentals=rows * SEQ_LEN * pairs * share,
        ),
        name="attention_forward",
    )(proj, *tables, *gain_rows)


def attention_backward(proj, tables, gain_rows, rot, logsums, grad_context, pairs, share):
    rows, width = proj.shape
    query_width = pairs * share * HEAD_DIM
    key_width = pairs * HEAD_DIM
    sequences = rows // SEQ_LEN
    return pl.pallas_call(
        functools.partial(backward_kernel, pairs, share, min(256, SEQ_LEN)),
        grid=(sequences,),
        in_specs=[
            row_spec(width), row_spec(128), row_spec(128),
            whole_spec(query_width), whole_spec(key_width),
            row_spec(width),
            pl.BlockSpec((8, SEQ_LEN), lambda sequence: (sequence, 0)),
            row_spec(query_width),
        ],
        out_specs=[
            row_spec(width),
            pl.BlockSpec((8, query_width + key_width), lambda sequence: (sequence, 0)),
        ],
        out_shape=[
            jax.ShapeDtypeStruct((rows, width), jnp.bfloat16),
            jax.ShapeDtypeStruct((sequences * 8, query_width + key_width), jnp.float32),
        ],
        scratch_shapes=[
            pltpu.VMEM((SEQ_LEN, query_width), jnp.float32),
            pltpu.VMEM((SEQ_LEN, key_width), jnp.float32),
            pltpu.VMEM((SEQ_LEN, key_width), jnp.float32),
        ],
        compiler_params=pltpu.CompilerParams(vmem_limit_bytes=48 * 1024 * 1024),
        cost_estimate=pl.CostEstimate(
            flops=10 * rows * SEQ_LEN * query_width,
            bytes_accessed=14 * rows * width,
            transcendentals=rows * SEQ_LEN * pairs * share,
        ),
        name="attention_backward",
    )(proj, *tables, *gain_rows, rot, logsums, grad_context)


def gather_tokens(rows):
    return lax.all_gather(rows, "tp", axis=0, tiled=True)


def scatter_tokens(partial):
    return lax.psum_scatter(
        partial.astype(jnp.bfloat16), "tp", scatter_dimension=0, tiled=True
    ).astype(jnp.float32)


def on_device(
    tokens,
    positions,
    first_gain,
    query_weight,
    key_weight,
    value_weight,
    query_gain,
    key_gain,
    out_weight,
    second_gain,
    gate_weight,
    up_weight,
    down_weight,
    cotangent,
):
    group_rows = positions.shape[0]
    heads_here = query_weight.shape[1] // HEAD_DIM
    pairs_here = key_weight.shape[1] // HEAD_DIM
    share = heads_here // pairs_here
    query_width = query_weight.shape[1]
    key_width = key_weight.shape[1]
    proj_width = query_width + 2 * key_width
    units = gate_weight.shape[1]
    attention_weights = lax.all_gather(
        jnp.concatenate([query_weight, key_weight, value_weight, out_weight.T], axis=1),
        "fsdp", axis=0, tiled=True,
    )
    unit_weights = lax.all_gather(
        jnp.concatenate([gate_weight, up_weight, down_weight.T], axis=1),
        "fsdp", axis=0, tiled=True,
    )
    whole_proj = attention_weights[:, :proj_width]
    whole_out = attention_weights[:, proj_width:]
    whole_gate = unit_weights[:, :units]
    whole_up = unit_weights[:, units : 2 * units]
    whole_down = unit_weights[:, 2 * units :]
    inputs = tokens.astype(jnp.float32)
    unit_one, inverse_one = normalize(inputs)
    normed_one = gather_tokens((unit_one * first_gain).astype(jnp.bfloat16))
    proj = dot_plain(normed_one, whole_proj)
    tables = angle_tables(positions)
    gain_rows = (
        jnp.tile(query_gain, heads_here)[None, :], jnp.tile(key_gain, pairs_here)[None, :]
    )
    rot, context, logsums = attention_forward(proj, tables, gain_rows, pairs_here, share)
    hidden = inputs + scatter_tokens(dot_cols(context, whole_out))
    unit_two, inverse_two = normalize(hidden)
    normed_two = gather_tokens((unit_two * second_gain).astype(jnp.bfloat16))
    grad_result = gather_tokens(cotangent)
    gate_value = dot_plain(normed_two, whole_gate)
    up_value = dot_plain(normed_two, whole_up)
    sigmoid_gate = jax.nn.sigmoid(gate_value)
    active = gate_value * sigmoid_gate
    mixed_units = (active * up_value).astype(jnp.bfloat16)
    grad_mixed = dot_plain(grad_result, whole_down)
    grad_gate = (
        grad_mixed * up_value * sigmoid_gate * (1.0 + gate_value * (1.0 - sigmoid_gate))
    ).astype(jnp.bfloat16)
    grad_up = (grad_mixed * active).astype(jnp.bfloat16)
    grad_normed_two = scatter_tokens(
        dot_cols(grad_gate, whole_gate) + dot_cols(grad_up, whole_up)
    )
    result = hidden + scatter_tokens(dot_cols(mixed_units, whole_down))
    output = result.astype(jnp.bfloat16)
    unit_grads = jnp.concatenate(
        [
            dot_rows(normed_two, grad_gate).astype(jnp.bfloat16),
            dot_rows(normed_two, grad_up).astype(jnp.bfloat16),
            dot_rows(grad_result, mixed_units).astype(jnp.bfloat16),
        ],
        axis=1,
    )
    grad_normed_two, unit_grads = lax.optimization_barrier((grad_normed_two, unit_grads))
    unit_shard = lax.psum_scatter(unit_grads, "fsdp", scatter_dimension=0, tiled=True)
    gain_two = jnp.sum(grad_normed_two * unit_two, axis=0)
    grad_hidden = cotangent.astype(jnp.float32) + norm_back(
        grad_normed_two * second_gain, unit_two, inverse_two
    )
    grad_hidden_all = gather_tokens(grad_hidden.astype(jnp.bfloat16))
    grad_context = dot_plain(grad_hidden_all, whole_out).astype(jnp.bfloat16)
    grad_proj, gain_sums = attention_backward(
        proj, tables, gain_rows, rot, logsums, grad_context, pairs_here, share
    )
    grad_normed_one = scatter_tokens(dot_cols(grad_proj, whole_proj))
    attention_grads = jnp.concatenate(
        [
            dot_rows(normed_one, grad_proj).astype(jnp.bfloat16),
            dot_rows(grad_hidden_all, context).astype(jnp.bfloat16),
        ],
        axis=1,
    )
    attention_shard = lax.psum_scatter(
        attention_grads, "fsdp", scatter_dimension=0, tiled=True
    ).astype(jnp.float32)
    gain_one = jnp.sum(grad_normed_one * unit_one, axis=0)
    grad_tokens = grad_hidden + norm_back(grad_normed_one * first_gain, unit_one, inverse_one)
    gain_sums = jnp.sum(gain_sums.reshape(-1, 8, query_width + key_width)[:, 0], axis=0)
    gain_query = jnp.sum(gain_sums[:query_width].reshape(heads_here, HEAD_DIM), axis=0)
    gain_key = jnp.sum(gain_sums[query_width:].reshape(pairs_here, HEAD_DIM), axis=0)
    width = first_gain.shape[0]
    gains = lax.psum(
        jnp.concatenate([gain_one, gain_two, gain_query, gain_key]), ("fsdp", "tp")
    )
    unit_shard = unit_shard.astype(jnp.float32)
    return (
        output,
        grad_tokens,
        gains[:width],
        attention_shard[:, :query_width],
        attention_shard[:, query_width : query_width + key_width],
        attention_shard[:, query_width + key_width : proj_width],
        gains[2 * width : 2 * width + HEAD_DIM],
        gains[2 * width + HEAD_DIM :],
        attention_shard[:, proj_width:].T,
        gains[width : 2 * width],
        unit_shard[:, :units],
        unit_shard[:, units : 2 * units],
        unit_shard[:, 2 * units :].T,
    )


def solution(mesh):
    return jax.shard_map(
        on_device,
        mesh=mesh,
        in_specs=(
            P(("fsdp", "tp"), None),
            P("fsdp"),
            P(),
            P("fsdp", "tp"),
            P("fsdp", "tp"),
            P("fsdp", "tp"),
            P(),
            P(),
            P("tp", "fsdp"),
            P(),
            P("fsdp", "tp"),
            P("fsdp", "tp"),
            P("tp", "fsdp"),
            P(("fsdp", "tp"), None),
        ),
        out_specs=(
            P(("fsdp", "tp"), None),
            P(("fsdp", "tp"), None),
            P(),
            P("fsdp", "tp"),
            P("fsdp", "tp"),
            P("fsdp", "tp"),
            P(),
            P(),
            P("tp", "fsdp"),
            P(),
            P("fsdp", "tp"),
            P("fsdp", "tp"),
            P("tp", "fsdp"),
        ),
        check_vma=False,
    )
```

time: 1470 us -> 817 us (0.56)
  waiting for transfers between devices: 880 us -> 545 us
  blocking collectives: 163 us -> 39.7 us
  matrix products: 226 us -> 114 us
  local copies, waits for them, and re-layouts: 96.4 us -> 22.3 us
  Pallas kernels: 0 us -> 41.8 us
  other arithmetic: 69.7 us -> 31.3 us
    reduce_scatter x11 -> x5, waiting for transfers between devices: 690 us -> 231 us  [the longest x1 128 us: on_device(): lax.psum_scatter(unit_grads, 'fsdp', scatter_dimension=0, tiled=True)]
    all_gather x4 -> x0, blocking collectives: 123 us -> none  [the longest x1 32.7 us: on_device(): lax.all_gather(key_weight, 'fsdp', axis=0, tiled=True)]
    dot_general x28 -> x0, matrix products: 85.2 us -> none  [the longest x4 23.4 us: one_sequence(): jnp.einsum('ikgd,jkd->kgij', grad_block, value_seq, preferred_element_typ...]
    all_gather x7 -> x6, waiting for transfers between devices: 187 us -> 265 us  [the longest x4 120 us: gather_tokens(): return lax.all_gather(rows, 'tp', axis=0, tiled=True)]
    dynamic_update_slice x8 -> x0, local copies, waits for them, and re-layouts: 60.8 us -> none  [the longest x4 39.7 us: attention_forward(): return lax.map(one_sequence, (query_rot, key_rot, value_proj))]
    unnamed x18 -> x13, waiting for transfers between devices: 2.65 us -> 48.7 us
    pallas_call x0 -> x2, Pallas kernels: none -> 41.8 us  [the longest x1 29.2 us: attention_backward(): pl.pallas_call(functools.partial(backward_kernel, pairs, share, min(256,...]
    convert_element_type x6 -> x7, other arithmetic: 37 us -> 7.97 us  [the longest x1 1.96 us: on_device(): normed_one = gather_tokens((unit_one * first_gain).astype(jnp.bfloat16))]
  transfers between devices with their start and end apart: 18 -> 12, of which waited for: 14 -> 12; matrix products, arithmetic and copies ran while one was open for 6% -> 12% of each run, Pallas kernels for 0% -> 0%
where the time goes in v1:
time: 817 us; the launch traced here: 810 us
  waiting for transfers between devices  545 us (67%)
  matrix products  114 us (14%)
  Pallas kernels  41.8 us (5%)
  blocking collectives  39.7 us (5%)
  other arithmetic  31.3 us (4%)
  local copies, waits for them, and re-layouts  22.3 us (3%)
  between operations  15.1 us (2%)
    reduce_scatter x1, waiting for transfers between devices, on_device(): lax.psum_scatter(unit_grads, 'fsdp', scatter_dimension=0, tiled=True)  128 us
    all_gather x4, waiting for transfers between devices, gather_tokens(): return lax.all_gather(rows, 'tp', axis=0, tiled=True)  120 us
    all_gather x1, waiting for transfers between devices, on_device(): lax.all_gather(jnp.concatenate([gate_weight, up_weight, down_weight.T], a...  107 us
    reduce_scatter x4, waiting for transfers between devices, scatter_tokens(): lax.psum_scatter(partial.astype(jnp.bfloat16), 'tp', scatter_dimension=0,...  103 us
    unnamed x13, waiting for transfers between devices  48.7 us
    dot_general x5, matrix products, dot_plain(): return jnp.dot(left, right, preferred_element_type=jnp.float32)  48.6 us
    psum x1, blocking collectives, on_device(): lax.psum(jnp.concatenate([gain_one, gain_two, gain_query, gain_key]), ('f...  39.7 us
    all_gather x1, waiting for transfers between devices, on_device(): lax.all_gather(jnp.concatenate([query_weight, key_weight, value_weight, o...  38.3 us
  transfers between devices with their start and end apart: 12, of which 12 were waited for; matrix products, arithmetic and copies ran while one was open for 12% of the time, Pallas kernels for 0%

profile of v1, /device:TPU:0, one launch (start us, length us, event | category | flops | bytes accessed | tf_op | source)
XLA Modules:
  0.0 809.7 jit_solution(14880135831331606233)
XLA Ops:
  10.1 1.5 pad_maximum_fusion.3
  11.7 1.5 fusion.16
  13.8 2.0 fusion.13
  16.0 3.7 fusion.33
  19.8 1.7 maximum_bitcast_fusion
  21.5 38.3 %all-gather.9.cloned.1.call-done = bf16[1024,768]{0,1:T(8,128)(2,1)} async-done(((bf16[128,768]{0,1:T(8,128)(2,1)}), bf16[1024,768]{0,1:T(8,128)(2,1)}) %all-gather.9.cloned.1.call-update) | async-done | bytes 1572880 | tf_op jit(solution)/shard_map/all_gather | solution.py:325
  59.8 34.8 %all-gather.7.cloned.1.call-done = bf16[2048,1024]{1,0:T(8,128)(2,1)} async-done(((bf16[512,1024]{1,0:T(8,128)(2,1)}), bf16[2048,1024]{1,0:T(8,128)(2,1)}) %all-gather.7.cloned.1.call-update) | async-done | bytes 4194320 | tf_op jit(solution)/shard_map/all_gather | solution.py:292
  94.6 6.9 fusion.29.proj_ref
  101.5 12.6 %attention_forward.1 = (bf16[2048,512]{1,0:T(8,128)(2,1)S(1)}, bf16[2048,256]{1,0:T(8,128)(2,1)S(1)}, f32[16,1024]{1,0:T(8,128)S(1)}) custom-call(f32[2048,512]{1,0:T(8,128)} %fusion.29.proj_ref, f32[2048,128]{1,0:T(8,128)S(1)} %get-tuple-element.99.cosine_ref, f32[2048,128]{1,0:T(8,128)S(1)} %get-tuple-element.100.sine_ref, ...), custom_call_target="tpu_custom_call" | custom-call | flops 2147483648 | bytes 10485760 | tf_op jit(solution)/shard_map/attention_forward/pallas_call | solution.py:226
  114.1 1.3 copy-done.2
  115.4 4.4 convolution_convert_fusion.5
  121.1 1.9 copy.65
  123.0 2.0 pad_maximum_fusion.2
  125.1 39.5 %reduce-scatter.9.cloned.1.call-done = bf16[512,1024]{1,0:T(8,128)(2,1)} async-done(((bf16[2048,1024]{1,0:T(8,128)(2,1)}), bf16[512,1024]{1,0:T(8,128)(2,1)}) %reduce-scatter.9.cloned.1.call-update) | async-done | bytes 1048592 | tf_op jit(solution)/shard_map/reduce_scatter | solution.py:296
  164.5 2.1 multiply_reduce_fusion.2
  166.7 1.4 multiply_convert_fusion.1
  168.7 107.4 %all-gather.13.cloned.1.call-done = bf16[1024,3456]{0,1:T(8,128)(2,1)} async-done(((bf16[128,3456]{0,1:T(8,128)(2,1)}), bf16[1024,3456]{0,1:T(8,128)(2,1)}) %all-gather.13.cloned.1.call-update) | async-done | bytes 7077904 | tf_op jit(solution)/shard_map/all_gather | solution.py:329
  276.1 34.8 %all-gather.11.cloned.1.call-done = bf16[2048,1024]{1,0:T(8,128)(2,1)} async-done(((bf16[512,1024]{1,0:T(8,128)(2,1)}), bf16[2048,1024]{1,0:T(8,128)(2,1)}) %all-gather.11.cloned.1.call-update) | async-done | bytes 4194320 | tf_op jit(solution)/shard_map/all_gather | solution.py:292
  310.9 10.9 %fusion.21 = f32[2048,1152]{1,0:T(8,128)} fusion(bf16[2048,1024]{1,0:T(8,128)(2,1)} %all-gather.11.cloned.1.call-done, bf16[1024,3456]{0,1:T(8,128)(2,1)} %all-gather.13.cloned.1.call-done), kind=kOutput, calls=%fused_computation.44 | convolution fusion | flops 4831838208 | bytes 15990784 | tf_op jit(solution)/shard_map/dot_general | solution.py:21
  321.8 9.7 %fusion.25 = f32[2048,1152]{1,0:T(8,128)} fusion(bf16[2048,1024]{1,0:T(8,128)(2,1)S(1)} %copy-done.19, bf16[1024,3456]{0,1:T(8,128)(2,1)} %all-gather.13.cloned.1.call-done), kind=kOutput, calls=%fused_computation.48 | convolution fusion | flops 4831838208 | bytes 15990784 | tf_op jit(solution)/shard_map/dot_general | solution.py:21
  331.5 15.4 %all-gather.15.cloned.1.call-done = bf16[2048,1024]{1,0:T(8,128)(2,1)} async-done(((bf16[512,1024]{1,0:T(8,128)(2,1)}), bf16[2048,1024]{1,0:T(8,128)(2,1)}) %all-gather.15.cloned.1.call-update) | async-done | bytes 4194320 | tf_op jit(solution)/shard_map/all_gather | solution.py:292
  346.9 17.5 %fusion.3 = (bf16[2048,1152]{1,0:T(8,128)(2,1)}, bf16[2048,1152]{1,0:T(8,128)(2,1)S(1)}, bf16[2048,1152]{1,0:T(8,128)(2,1)}) fusion(f32[2048,1152]{1,0:T(8,128)} %fusion.25, f32[2048,1152]{1,0:T(8,128)} %fusion.21, bf16[2048,1024]{1,0:T(8,128)(2,1)} %all-gather.15.cloned.1.call-done, bf16[1024,3456]{0,1:T(8,128)(2,1)} %all-gather.13.cloned.1.call-done), kind=kOutput, calls=%fused_computation.5 | convolution fusion | flops 4867227648 | bytes 39583744 | tf_op jit(solution)/shard_map/dot_general | solution.py:21
  364.4 9.1 %fusion.23 = f32[2048,1024]{1,0:T(8,128)S(1)} fusion(bf16[2048,1152]{1,0:T(8,128)(2,1)S(1)} %get-tuple-element.84, bf16[1024,3456]{0,1:T(8,128)(2,1)} %all-gather.13.cloned.1.call-done), kind=kOutput, calls=%fused_computation.46 | convolution fusion | flops 4831838208 | bytes 15466496 | tf_op jit(solution)/shard_map/dot_general | solution.py:31
  373.5 8.8 %add_convert_fusion = bf16[2048,1024]{1,0:T(8,128)(2,1)} fusion(f32[2048,1024]{1,0:T(8,128)S(1)} %fusion.23, bf16[2048,1152]{1,0:T(8,128)(2,1)S(1)} %copy-done.25, bf16[1024,3456]{0,1:T(8,128)(2,1)} %all-gather.13.cloned.1.call-done), kind=kOutput, calls=%fused_computation.9 | convolution fusion | flops 4836032512 | bytes 19660800 | tf_op jit(solution)/shard_map/dot_general | solution.py:31
  382.5 9.2 %convolution_convert_fusion.2 = bf16[1024,1152]{1,0:T(8,128)(2,1)S(1)} fusion(bf16[2048,1024]{1,0:T(8,128)(2,1)} %all-gather.11.cloned.1.call-done, bf16[2048,1152]{1,0:T(8,128)(2,1)} %get-tuple-element.83), kind=kOutput, calls=%fused_computation.13 | convolution fusion | flops 4833017856 | bytes 11272192 | tf_op jit(solution)/shard_map/dot_general | solution.py:25
  391.7 8.7 %convolution_convert_fusion.3 = bf16[1024,1152]{1,0:T(8,128)(2,1)S(1)} fusion(bf16[2048,1024]{1,0:T(8,128)(2,1)S(1)} %copy-done.20, bf16[2048,1152]{1,0:T(8,128)(2,1)} %copy-done.24), kind=kOutput, calls=%fused_computation.14 | convolution fusion | flops 4833017856 | bytes 11272192 | tf_op jit(solution)/shard_map/dot_general | solution.py:25
  400.5 6.0 fusion.5
  406.5 3.3 pad_maximum_fusion
  409.8 17.3 %reduce-scatter.13.cloned.1.call-done = bf16[512,1024]{1,0:T(8,128)(2,1)} async-done(((bf16[2048,1024]{1,0:T(8,128)(2,1)}), bf16[512,1024]{1,0:T(8,128)(2,1)}) %reduce-scatter.13.cloned.1.call-update) | async-done | bytes 1048592 | tf_op jit(solution)/shard_map/reduce_scatter | solution.py:296
  427.1 1.6 convert_element_type.95
  430.9 1.7 fusion.34
  432.7 34.6 %all-gather.17.cloned.1.call-done = bf16[2048,1024]{1,0:T(8,128)(2,1)} async-done(((bf16[512,1024]{1,0:T(8,128)(2,1)}), bf16[2048,1024]{1,0:T(8,128)(2,1)}) %all-gather.17.cloned.1.call-update) | async-done | bytes 4194320 | tf_op jit(solution)/shard_map/all_gather | solution.py:292
  467.3 3.6 convolution_convert_fusion.6.grad_context_ref
  470.9 29.2 %attention_backward.1 = (bf16[2048,512]{1,0:T(8,128)(2,1)S(1)}, f32[16,384]{1,0:T(8,128)S(1)}) custom-call(f32[2048,512]{1,0:T(8,128)} %fusion.29.proj_ref, f32[2048,128]{1,0:T(8,128)S(1)} %get-tuple-element.99.cosine_ref, f32[2048,128]{1,0:T(8,128)S(1)} %get-tuple-element.100.sine_ref, f32[1,256]{1,0:T(1,128)S(1)} %broadcast_in_dim_tile.6.query_gain_ref, ...), custom_call_target="tpu_custom_call" | custom-call | flops 5368709120 | bytes 14680064 | tf_op jit(solution)/shard_map/attention_backward/pallas_call | solution.py:258
  500.1 1.3 convolution_convert_fusion.8
  501.5 1.6 copy-done.18
  503.1 2.4 convolution_convert_fusion.7
  505.6 1.6 copy.74
  508.8 5.6 convolution_convert_fusion
  514.5 9.9 %convolution_convert_fusion.4 = bf16[2048,1024]{1,0:T(8,128)(2,1)} fusion(bf16[2048,1152]{1,0:T(8,128)(2,1)} %get-tuple-element.85, bf16[1024,3456]{0,1:T(8,128)(2,1)} %all-gather.13.cloned.1.call-done), kind=kOutput, calls=%fused_computation.15 | convolution fusion | flops 4833935360 | bytes 11272192 | tf_op jit(solution)/shard_map/dot_general | solution.py:31
  524.7 47.5 %reduce-scatter.19.cloned.1.call-done = bf16[128,768]{1,0:T(8,128)(2,1)} async-done(((bf16[1024,768]{1,0:T(8,128)(2,1)}), bf16[128,768]{1,0:T(8,128)(2,1)}) %reduce-scatter.19.cloned.1.call-update) | async-done | bytes 196624
  576.2 127.9 %reduce-scatter.17.cloned.1.call-done = bf16[128,3456]{1,0:T(8,128)(2,1)} async-done(((bf16[1024,3456]{1,0:T(8,128)(2,1)}), bf16[128,3456]{1,0:T(8,128)(2,1)}) %reduce-scatter.17.cloned.1.call-update) | async-done | bytes 884752 | tf_op jit(solution)/shard_map/reduce_scatter | solution.py:375
  706.5 2.3 fusion.35
  708.8 41.4 %reduce-scatter.15.cloned.1.call-done = bf16[512,1024]{1,0:T(8,128)(2,1)} async-done(((bf16[2048,1024]{1,0:T(8,128)(2,1)}), bf16[512,1024]{1,0:T(8,128)(2,1)}) %reduce-scatter.15.cloned.1.call-update) | async-done | bytes 1048592 | tf_op jit(solution)/shard_map/reduce_scatter | solution.py:296
  750.2 2.0 fusion.15
  752.3 39.7 %psum.7 = f32[2176]{0:T(1024)S(1)} all-reduce(f32[2176]{0:T(1024)S(1)} %concatenate.26), channel_id=1, replica_groups=mesh['fsdp'=8,'tp'=4] {'fsdp','tp'}, use_global_device_ids=true, to_apply=%region_13.0 | all-reduce | flops 2176 | bytes 17408 | tf_op jit(solution)/shard_map/psum | solution.py:402
  793.2 4.8 reduce-scatter.11.cloned.1.call-done
  798.0 4.4 fusion.12
  (116 shorter events, 17.7 us)
Async XLA Ops:
  7.2 6.6 copy-start.3
  7.2 52.6 %all-gather.9.cloned.1.call-start = ((), (), s32[]{:S(2)}) async-start(), calls=%async_computation.7 | async-start | bytes 1769472 | tf_op jit(solution)/shard_map/all_gather | solution.py:325
  10.0 5.8 copy-start.23
  10.0 5.9 copy-start.17
  10.0 6.0 copy-start.16
  11.6 83.0 %all-gather.7.cloned.1.call-start = ((), (), s32[]{:S(2)}) async-start(), calls=%async_computation.6 | async-start | bytes 5242880 | tf_op jit(solution)/shard_map/all_gather | solution.py:292
  13.2 0.6 copy-start.14
  15.8 148.8 %reduce-scatter.9.cloned.1.call-start = ((), (), s32[]{:S(2)}) async-start(), calls=%async_computation.8 | async-start | bytes 5242880 | tf_op jit(solution)/shard_map/reduce_scatter | solution.py:296
  114.1 1.3 copy-start.2
  119.9 156.3 %all-gather.13.cloned.1.call-start = ((), (), s32[]{:S(2)}) async-start(), calls=%async_computation.10 | async-start | bytes 7962624 | tf_op jit(solution)/shard_map/all_gather | solution.py:329
  122.9 43.7 %copy-start.12 = (f32[1024]{0:T(1024)S(1)}, f32[1024]{0:T(1024)}, u32[]{:S(2)}) copy-start(f32[1024]{0:T(1024)} %param.23) | copy-start | bytes 12292
  125.0 185.9 %all-gather.11.cloned.1.call-start = ((), (), s32[]{:S(2)}) async-start(), calls=%async_computation.9 | async-start | bytes 5242880 | tf_op jit(solution)/shard_map/all_gather | solution.py:292
  164.5 2.1 copy-start.4
  164.5 2.2 copy-start.9
  168.1 178.8 %all-gather.15.cloned.1.call-start = ((), (), s32[]{:S(2)}) async-start(), calls=%async_computation.12 | async-start | bytes 5242880 | tf_op jit(solution)/shard_map/all_gather | solution.py:292
  168.7 258.4 %reduce-scatter.13.cloned.1.call-start = ((), (), s32[]{:S(2)}) async-start(), calls=%async_computation.13 | async-start | bytes 5242880 | tf_op jit(solution)/shard_map/reduce_scatter | solution.py:296
  310.9 10.9 %copy-start.19 = (bf16[2048,1024]{1,0:T(8,128)(2,1)S(1)}, bf16[2048,1024]{1,0:T(8,128)(2,1)}, u32[]{:S(2)}) copy-start(bf16[2048,1024]{1,0:T(8,128)(2,1)} %all-gather.11.cloned.1.call-done) | copy-start | bytes 12582916
  364.4 9.2 %copy-start.24 = (bf16[2048,1152]{1,0:T(8,128)(2,1)}, bf16[2048,1152]{1,0:T(8,128)(2,1)S(1)}, u32[]{:S(2)}) copy-start(bf16[2048,1152]{1,0:T(8,128)(2,1)S(1)} %get-tuple-element.84) | copy-start | bytes 14155780
  364.4 9.2 %copy-start.25 = (bf16[2048,1152]{1,0:T(8,128)(2,1)S(1)}, bf16[2048,1152]{1,0:T(8,128)(2,1)}, u32[]{:S(2)}) copy-start(bf16[2048,1152]{1,0:T(8,128)(2,1)} %get-tuple-element.83) | copy-start | bytes 14155780
  382.4 84.9 %all-gather.17.cloned.1.call-start = ((), (), s32[]{:S(2)}) async-start(), calls=%async_computation.14 | async-start | bytes 5242880 | tf_op jit(solution)/shard_map/all_gather | solution.py:292
  382.5 9.2 %copy-start.20 = (bf16[2048,1024]{1,0:T(8,128)(2,1)S(1)}, bf16[2048,1024]{1,0:T(8,128)(2,1)}, u32[]{:S(2)}) copy-start(bf16[2048,1024]{1,0:T(8,128)(2,1)} %all-gather.11.cloned.1.call-done) | copy-start | bytes 12582916
  382.5 18.0 %slice-start = ((s8[4718592]{0:T(1024)(128)(4,1)}), s8[4194304]{0:T(1024)(128)(4,1)S(1)}, s32[]{:S(2)}) async-start(s8[4718592]{0:T(1024)(128)(4,1)} %bitcast.48), calls=%async_computation.18 | async-start | bytes 8388608
  391.7 8.8 %copy-start.21 = (bf16[2048,1024]{1,0:T(8,128)(2,1)S(1)}, bf16[2048,1024]{1,0:T(8,128)(2,1)}, u32[]{:S(2)}) copy-start(bf16[2048,1024]{1,0:T(8,128)(2,1)} %all-gather.15.cloned.1.call-done) | copy-start | bytes 12582916
  391.7 8.8 %slice-start.1 = ((s8[4718592]{0:T(1024)(128)(4,1)}), s8[524288]{0:T(1024)(128)(4,1)S(1)}, s32[]{:S(2)}) async-start(s8[4718592]{0:T(1024)(128)(4,1)} %bitcast.48), calls=%async_computation.19 | async-start | bytes 1048576
  427.1 1.6 copy-start.5
  427.1 1.9 copy-start.10
  428.9 1.3 copy-start.7
  428.9 2.0 copy-start.11
  432.7 139.5 %reduce-scatter.19.cloned.1.call-start = ((), (), s32[]{:S(2)}) async-start(), calls=%async_computation.17 | async-start | bytes 1769472
  470.9 29.2 %copy-start.22 = (bf16[2048,1024]{1,0:T(8,128)(2,1)S(1)}, bf16[2048,1024]{1,0:T(8,128)(2,1)}, u32[]{:S(2)}) copy-start(bf16[2048,1024]{1,0:T(8,128)(2,1)} %all-gather.17.cloned.1.call-done) | copy-start | bytes 12582916
  500.1 1.3 copy-start
  500.1 2.9 copy-start.18
  507.2 1.6 copy-start.1
  507.2 196.9 %reduce-scatter.17.cloned.1.call-start = ((), (), s32[]{:S(2)}) async-start(), calls=%async_computation.16 | async-start | bytes 7962624 | tf_op jit(solution)/shard_map/reduce_scatter | solution.py:375
  507.8 242.4 %reduce-scatter.15.cloned.1.call-start = ((), (), s32[]{:S(2)}) async-start(), calls=%async_computation.15 | async-start | bytes 5242880 | tf_op jit(solution)/shard_map/reduce_scatter | solution.py:296
  514.4 283.6 %reduce-scatter.11.cloned.1.call-start = ((), (), s32[]{:S(2)}) async-start(), calls=%async_computation.11 | async-start | bytes 5242880 | tf_op jit(solution)/shard_map/reduce_scatter | solution.py:296
  705.4 44.8 %copy-start.6 = (bf16[512,1024]{1,0:T(8,128)(2,1)S(1)}, bf16[512,1024]{1,0:T(8,128)(2,1)}, u32[]{:S(2)}) copy-start(bf16[512,1024]{1,0:T(8,128)(2,1)} %param.14) | copy-start | bytes 3145732
  705.4 44.8 %copy-start.13 = (f32[1024]{0:T(1024)S(1)}, f32[1024]{0:T(1024)}, u32[]{:S(2)}) copy-start(f32[1024]{0:T(1024)} %param.16) | copy-start | bytes 12292
  705.4 44.8 %copy-start.15 = (f32[512]{0:T(512)S(1)}, f32[512]{0:T(512)}, u32[]{:S(2)}) copy-start(f32[512]{0:T(512)} %copy-done.14) | copy-start | bytes 6148
  706.5 91.5 %copy-start.8 = (f32[512,1024]{1,0:T(8,128)S(1)}, f32[512,1024]{1,0:T(8,128)}, u32[]{:S(2)}) copy-start(f32[512,1024]{1,0:T(8,128)} %copy-done.7) | copy-start | bytes 6291460
Sparse Core Ops, SparseCore 0:
  11.8 47.9 all-gather.8
  61.9 32.6 all-gather.6
  120.0 44.4 reduce-scatter.8
  166.6 109.4 all-gather.12
  278.2 32.6 all-gather.10
  312.4 34.4 all-gather.14
  382.5 44.5 reduce-scatter.12
  432.8 34.4 all-gather.16
  507.3 64.7 reduce-scatter.18
  576.1 127.9 reduce-scatter.16
  706.6 43.5 reduce-scatter.14
  752.7 45.2 reduce-scatter.10

commit v2 on v1

--- a/solution.py
+++ b/solution.py
@@ -280,22 +280,231 @@
         ],
         compiler_params=pltpu.CompilerParams(vmem_limit_bytes=48 * 1024 * 1024),
         cost_estimate=pl.CostEstimate(
-            flops=10 * rows * SEQ_LEN * query_width,
-            bytes_accessed=14 * rows * width,
-            transcendentals=rows * SEQ_LEN * pairs * share,
+            flops=2 * rows * width,
+            bytes_accessed=rows * width,
+            transcendentals=0,
         ),
         name="attention_backward",
     )(proj, *tables, *gain_rows, rot, logsums, grad_context)
 
 
-def gather_tokens(rows):
-    return lax.all_gather(rows, "tp", axis=0, tiled=True)
-
-
-def scatter_tokens(partial):
-    return lax.psum_scatter(
-        partial.astype(jnp.bfloat16), "tp", scatter_dimension=0, tiled=True
-    ).astype(jnp.float32)
+MESH_ID = pl.DeviceIdType.MESH
+CHUNKS = 4
+
+
+def greet(peers):
+    barrier = pltpu.get_barrier_semaphore()
+    for peer in peers:
+        pl.semaphore_signal(barrier, inc=1, device_id=peer, device_id_type=MESH_ID)
+    pl.semaphore_wait(barrier, len(peers))
+
+
+def tp_partners():
+    me = lax.axis_index("tp")
+    near = me + 1 - 2 * lax.rem(me, 2)
+    far = lax.rem(me + 2, 4)
+    return (me, near, far)
+
+
+def gather_kernel(
+    rows_ref, whole_ref, local_sem, near_send, near_recv, far_send, far_recv, pass_send, pass_recv
+):
+    me, near, far = tp_partners()
+    rows = rows_ref.shape[0]
+    step = rows // CHUNKS
+
+    def remote(source, target, sends, recvs, chunk, peer):
+        return pltpu.make_async_remote_copy(
+            src_ref=source, dst_ref=target, send_sem=sends.at[chunk], recv_sem=recvs.at[chunk],
+            device_id={"tp": peer}, device_id_type=MESH_ID,
+        )
+
+    greet([{"tp": near}, {"tp": far}])
+    far_copies = []
+    near_copies = []
+    for chunk in range(CHUNKS):
+        source = rows_ref.at[pl.ds(chunk * step, step)]
+        target = whole_ref.at[pl.ds(pl.multiple_of(me * rows + chunk * step, step), step)]
+        far_copies.append(remote(source, target, far_send, far_recv, chunk, far))
+        far_copies[-1].start()
+    for chunk in range(CHUNKS):
+        source = rows_ref.at[pl.ds(chunk * step, step)]
+        target = whole_ref.at[pl.ds(pl.multiple_of(me * rows + chunk * step, step), step)]
+        near_copies.append(remote(source, target, near_send, near_recv, chunk, near))
+        near_copies[-1].start()
+    local = pltpu.make_async_copy(
+        rows_ref, whole_ref.at[pl.ds(pl.multiple_of(me * rows, rows), rows)], local_sem
+    )
+    local.start()
+    pass_copies = []
+    for chunk in range(CHUNKS):
+        far_copies[chunk].wait_recv()
+        block = whole_ref.at[pl.ds(pl.multiple_of(far * rows + chunk * step, step), step)]
+        pass_copies.append(remote(block, block, pass_send, pass_recv, chunk, near))
+        pass_copies[-1].start()
+    for chunk in range(CHUNKS):
+        far_copies[chunk].wait_send()
+        near_copies[chunk].wait()
+    for chunk in range(CHUNKS):
+        pass_copies[chunk].wait()
+    local.wait()
+
+
+def gather_tokens(rows, collective_id):
+    count, width = rows.shape
+    return pl.pallas_call(
+        gather_kernel,
+        in_specs=[pl.BlockSpec(memory_space=pl.ANY)],
+        out_specs=pl.BlockSpec(memory_space=pl.ANY),
+        out_shape=jax.ShapeDtypeStruct((4 * count, width), rows.dtype),
+        scratch_shapes=[pltpu.SemaphoreType.DMA]
+        + [pltpu.SemaphoreType.DMA((CHUNKS,)) for _ in range(6)],
+        compiler_params=pltpu.CompilerParams(collective_id=collective_id, has_side_effects=True),
+        cost_estimate=pl.CostEstimate(
+            flops=2 * count * width, bytes_accessed=count * width, transcendentals=0
+        ),
+        name="gather_tokens",
+    )(rows)
+
+
+def scatter_kernel(
+    partial_ref, sum_ref, first_slot, second_slot, onward, arrived,
+    first_send, first_recv, second_send, second_recv, far_send, far_recv,
+):
+    me, near, far = tp_partners()
+    opposite = lax.rem(near + 2, 4)
+    rows = sum_ref.shape[0]
+    step = rows // CHUNKS
+
+    def remote(source, target, sends, recvs, chunk, peer):
+        return pltpu.make_async_remote_copy(
+            src_ref=source, dst_ref=target, send_sem=sends.at[chunk], recv_sem=recvs.at[chunk],
+            device_id={"tp": peer}, device_id_type=MESH_ID,
+        )
+
+    def block(owner, chunk):
+        return pl.ds(pl.multiple_of(owner * rows + chunk * step, step), step)
+
+    greet([{"tp": near}, {"tp": far}])
+    first_copies = []
+    second_copies = []
+    far_copies = []
+    for chunk in range(CHUNKS):
+        first_copies.append(
+            remote(
+                partial_ref.at[block(opposite, chunk)],
+                first_slot.at[pl.ds(chunk * step, step)],
+                first_send, first_recv, chunk, near,
+            )
+        )
+        first_copies[-1].start()
+    for chunk in range(CHUNKS):
+        second_copies.append(
+            remote(
+                partial_ref.at[block(near, chunk)],
+                second_slot.at[pl.ds(chunk * step, step)],
+                second_send, second_recv, chunk, near,
+            )
+        )
+        second_copies[-1].start()
+    for chunk in range(CHUNKS):
+        here = pl.ds(chunk * step, step)
+        first_copies[chunk].wait_recv()
+        onward[here, :] = (
+            partial_ref[block(far, chunk), :].astype(jnp.float32)
+            + first_slot[here, :].astype(jnp.float32)
+        ).astype(jnp.bfloat16)
+        far_copies.append(
+            remote(onward.at[here], arrived.at[here], far_send, far_recv, chunk, far)
+        )
+        far_copies[-1].start()
+    for chunk in range(CHUNKS):
+        here = pl.ds(chunk * step, step)
+        second_copies[chunk].wait_recv()
+        far_copies[chunk].wait_recv()
+        sum_ref[here, :] = (
+            partial_ref[block(me, chunk), :].astype(jnp.float32)
+            + second_slot[here, :].astype(jnp.float32)
+            + arrived[here, :].astype(jnp.float32)
+        )
+    for chunk in range(CHUNKS):
+        first_copies[chunk].wait_send()
+        second_copies[chunk].wait_send()
+        far_copies[chunk].wait_send()
+
+
+def scatter_tokens(partial, collective_id):
+    partial = partial.astype(jnp.bfloat16)
+    count, width = partial.shape[0] // 4, partial.shape[1]
+    return pl.pallas_call(
+        scatter_kernel,
+        in_specs=[pl.BlockSpec(memory_space=pltpu.VMEM)],
+        out_specs=pl.BlockSpec(memory_space=pltpu.VMEM),
+        out_shape=jax.ShapeDtypeStruct((count, width), jnp.float32),
+        scratch_shapes=[pltpu.VMEM((count, width), jnp.bfloat16) for _ in range(4)]
+        + [pltpu.SemaphoreType.DMA((CHUNKS,)) for _ in range(6)],
+        compiler_params=pltpu.CompilerParams(
+            collective_id=collective_id, has_side_effects=True, vmem_limit_bytes=32 * 1024 * 1024
+        ),
+        cost_estimate=pl.CostEstimate(
+            flops=2 * count * width, bytes_accessed=count * width, transcendentals=0
+        ),
+        name="scatter_tokens",
+    )(partial)
+
+
+def gains_kernel(
+    sizes, part_ref, sum_ref, tp_slots, fsdp_slots, tp_send, tp_recv, fsdp_send, fsdp_recv
+):
+    stages = (
+        ("tp", sizes[0], tp_slots, tp_send, tp_recv),
+        ("fsdp", sizes[1], fsdp_slots, fsdp_send, fsdp_recv),
+    )
+    greet(
+        [
+            {axis: lax.rem(lax.axis_index(axis) + offset, size)}
+            for axis, size, _, _, _ in stages
+            for offset in range(1, size)
+        ]
+    )
+    current = part_ref[...]
+    for axis, size, slots, sends, recvs in stages:
+        me = lax.axis_index(axis)
+        slots[me] = current
+        copies = []
+        for offset in range(1, size):
+            copies.append(
+                pltpu.make_async_remote_copy(
+                    src_ref=slots.at[me], dst_ref=slots.at[me],
+                    send_sem=sends.at[offset], recv_sem=recvs.at[offset],
+                    device_id={axis: lax.rem(me + offset, size)}, device_id_type=MESH_ID,
+                )
+            )
+            copies[-1].start()
+        for copy in copies:
+            copy.wait()
+        current = slots[0]
+        for source in range(1, size):
+            current = current + slots[source]
+    sum_ref[...] = current
+
+
+def sum_gains(values, collective_id):
+    sizes = (lax.axis_size("tp"), lax.axis_size("fsdp"))
+    length = values.shape[0]
+    rows = -(-length // 1024) * 8
+    part = jnp.pad(values, (0, rows * 128 - length)).reshape(rows, 128)
+    total = pl.pallas_call(
+        functools.partial(gains_kernel, sizes),
+        in_specs=[pl.BlockSpec(memory_space=pltpu.VMEM)],
+        out_specs=pl.BlockSpec(memory_space=pltpu.VMEM),
+        out_shape=jax.ShapeDtypeStruct((rows, 128), jnp.float32),
+        scratch_shapes=[pltpu.VMEM((size, rows, 128), jnp.float32) for size in sizes]
+        + [pltpu.SemaphoreType.DMA((size,)) for size in sizes for _ in range(2)],
+        compiler_params=pltpu.CompilerParams(collective_id=collective_id, has_side_effects=True),
+        name="sum_gains",
+    )(part)
+    return total.reshape(rows * 128)[:length]
 
 
 def on_device(
@@ -337,32 +546,33 @@
     whole_down = unit_weights[:, 2 * units :]
     inputs = tokens.astype(jnp.float32)
     unit_one, inverse_one = normalize(inputs)
-    normed_one = gather_tokens((unit_one * first_gain).astype(jnp.bfloat16))
+    normed_one = gather_tokens((unit_one * first_gain).astype(jnp.bfloat16), 1)
     proj = dot_plain(normed_one, whole_proj)
     tables = angle_tables(positions)
     gain_rows = (
         jnp.tile(query_gain, heads_here)[None, :], jnp.tile(key_gain, pairs_here)[None, :]
     )
     rot, context, logsums = attention_forward(proj, tables, gain_rows, pairs_here, share)
-    hidden = inputs + scatter_tokens(dot_cols(context, whole_out))
+    hidden = inputs + scatter_tokens(dot_cols(context, whole_out), 2)
     unit_two, inverse_two = normalize(hidden)
-    normed_two = gather_tokens((unit_two * second_gain).astype(jnp.bfloat16))
-    grad_result = gather_tokens(cotangent)
+    normed_two = gather_tokens((unit_two * second_gain).astype(jnp.bfloat16), 1)
+    grad_result = lax.all_gather(cotangent, "tp", axis=0, tiled=True)
     gate_value = dot_plain(normed_two, whole_gate)
     up_value = dot_plain(normed_two, whole_up)
     sigmoid_gate = jax.nn.sigmoid(gate_value)
     active = gate_value * sigmoid_gate
     mixed_units = (active * up_value).astype(jnp.bfloat16)
+    down_partial = dot_cols(mixed_units, whole_down).astype(jnp.bfloat16)
+    down_partial, grad_result = lax.optimization_barrier((down_partial, grad_result))
     grad_mixed = dot_plain(grad_result, whole_down)
     grad_gate = (
         grad_mixed * up_value * sigmoid_gate * (1.0 + gate_value * (1.0 - sigmoid_gate))
     ).astype(jnp.bfloat16)
     grad_up = (grad_mixed * active).astype(jnp.bfloat16)
     grad_normed_two = scatter_tokens(
-        dot_cols(grad_gate, whole_gate) + dot_cols(grad_up, whole_up)
-    )
-    result = hidden + scatter_tokens(dot_cols(mixed_units, whole_down))
-    output = result.astype(jnp.bfloat16)
+        dot_cols(grad_gate, whole_gate) + dot_cols(grad_up, whole_up), 2
+    )
+    down_sum = lax.psum_scatter(down_partial, "tp", scatter_dimension=0, tiled=True)
     unit_grads = jnp.concatenate(
         [
             dot_rows(normed_two, grad_gate).astype(jnp.bfloat16),
@@ -371,18 +581,21 @@
         ],
         axis=1,
     )
-    grad_normed_two, unit_grads = lax.optimization_barrier((grad_normed_two, unit_grads))
+    grad_normed_two, unit_grads, down_sum = lax.optimization_barrier(
+        (grad_normed_two, unit_grads, down_sum)
+    )
+    output = (hidden + down_sum.astype(jnp.float32)).astype(jnp.bfloat16)
     unit_shard = lax.psum_scatter(unit_grads, "fsdp", scatter_dimension=0, tiled=True)
     gain_two = jnp.sum(grad_normed_two * unit_two, axis=0)
     grad_hidden = cotangent.astype(jnp.float32) + norm_back(
         grad_normed_two * second_gain, unit_two, inverse_two
     )
-    grad_hidden_all = gather_tokens(grad_hidden.astype(jnp.bfloat16))
+    grad_hidden_all = gather_tokens(grad_hidden.astype(jnp.bfloat16), 1)
     grad_context = dot_plain(grad_hidden_all, whole_out).astype(jnp.bfloat16)
     grad_proj, gain_sums = attention_backward(
         proj, tables, gain_rows, rot, logsums, grad_context, pairs_here, share
     )
-    grad_normed_one = scatter_tokens(dot_cols(grad_proj, whole_proj))
+    grad_normed_one = scatter_tokens(dot_cols(grad_proj, whole_proj), 2)
     attention_grads = jnp.concatenate(
         [
             dot_rows(normed_one, grad_proj).astype(jnp.bfloat16),
@@ -390,6 +603,7 @@
         ],
         axis=1,
     )
+    attention_grads, unit_shard = lax.optimization_barrier((attention_grads, unit_shard))
     attention_shard = lax.psum_scatter(
         attention_grads, "fsdp", scatter_dimension=0, tiled=True
     ).astype(jnp.float32)
@@ -399,9 +613,7 @@
     gain_query = jnp.sum(gain_sums[:query_width].reshape(heads_here, HEAD_DIM), axis=0)
     gain_key = jnp.sum(gain_sums[query_width:].reshape(pairs_here, HEAD_DIM), axis=0)
     width = first_gain.shape[0]
-    gains = lax.psum(
-        jnp.concatenate([gain_one, gain_two, gain_query, gain_key]), ("fsdp", "tp")
-    )
+    gains = sum_gains(jnp.concatenate([gain_one, gain_two, gain_query, gain_key]), 3)
     unit_shard = unit_shard.astype(jnp.float32)
     return (
         output,

time: 817 us -> 509 us (0.62)
  waiting for transfers between devices: 545 us -> 87.3 us
  Pallas kernels: 41.8 us -> 242 us
  blocking collectives: 39.7 us -> 0 us
    pallas_call x0 -> x7, Pallas kernels: none -> 201 us  [the longest x3 104 us: gather_tokens(): pl.pallas_call(gather_kernel, in_specs=[pl.BlockSpec(memory_space=pl.ANY)...]
    all_gather x4 -> x1, waiting for transfers between devices: 120 us -> 3.62 us  [on_device(): grad_result = lax.all_gather(cotangent, 'tp', axis=0, tiled=True)]
    reduce_scatter x4 -> x1, waiting for transfers between devices: 103 us -> 0.01 us  [on_device(): lax.psum_scatter(down_partial, 'tp', scatter_dimension=0, tiled=True)]
    all_gather x1, waiting for transfers between devices: 107 us -> 22.5 us  [on_device(): lax.all_gather(jnp.concatenate([gate_weight, up_weight, down_weight.T], a...]
    reduce_scatter x1, waiting for transfers between devices: 128 us -> 49.2 us  [on_device(): lax.psum_scatter(unit_grads, 'fsdp', scatter_dimension=0, tiled=True)]
    psum x1 -> x0, blocking collectives: 39.7 us -> none  [on_device(): lax.psum(jnp.concatenate([gain_one, gain_two, gain_query, gain_key]), ('f...]
    all_gather x1, waiting for transfers between devices: 38.3 us -> 0.02 us  [on_device(): lax.all_gather(jnp.concatenate([query_weight, key_weight, value_weight, o...]
    unnamed x13 -> x7, waiting for transfers between devices: 48.7 us -> 11.9 us
  transfers between devices with their start and end apart: 12 -> 6, of which waited for: 12 -> 4; matrix products, arithmetic and copies ran while one was open for 12% -> 28% of each run, Pallas kernels for 0% -> 48%
where the time goes in v2:
time: 509 us; the launch traced here: 502 us
  Pallas kernels  242 us (48%)
  matrix products  106 us (21%)
  waiting for transfers between devices  87.3 us (17%)
  other arithmetic  26.1 us (5%)
  local copies, waits for them, and re-layouts  24.5 us (5%)
  between operations  15.3 us (3%)
    pallas_call x3, Pallas kernels, gather_tokens(): pl.pallas_call(gather_kernel, in_specs=[pl.BlockSpec(memory_space=pl.ANY)...  104 us
    pallas_call x3, Pallas kernels, scatter_tokens(): pl.pallas_call(scatter_kernel, in_specs=[pl.BlockSpec(memory_space=pltpu....  87.1 us
    reduce_scatter x1, waiting for transfers between devices, on_device(): lax.psum_scatter(unit_grads, 'fsdp', scatter_dimension=0, tiled=True)  49.2 us
    dot_general x5, matrix products, dot_plain(): return jnp.dot(left, right, preferred_element_type=jnp.float32)  47.3 us
    dot_general x5, matrix products, dot_cols(): lax.dot_general(left, right, (((1,), (1,)), ((), ())), preferred_element_...  34.3 us
    pallas_call x1, Pallas kernels, attention_backward(): pl.pallas_call(functools.partial(backward_kernel, pairs, share, min(256,...  28.9 us
    dot_general x5, matrix products, dot_rows(): lax.dot_general(left, right, (((0,), (0,)), ((), ())), preferred_element_...  24.5 us
    all_gather x1, waiting for transfers between devices, on_device(): lax.all_gather(jnp.concatenate([gate_weight, up_weight, down_weight.T], a...  22.5 us
  transfers between devices with their start and end apart: 6, of which 4 were waited for; matrix products, arithmetic and copies ran while one was open for 28% of the time, Pallas kernels for 48%

profile of v2, /device:TPU:0, one launch (start us, length us, event | category | flops | bytes accessed | tf_op | source)
XLA Modules:
  0.0 501.9 jit_solution(14088655337710314049)
XLA Ops:
  10.1 1.5 pad_maximum_fusion.3
  11.7 1.2 copy.58
  12.8 1.2 copy.59
  14.0 1.9 pad_maximum_fusion.2
  17.3 1.3 fusion.5.rows_ref
  18.6 36.0 %gather_tokens.3 = bf16[2048,1024]{1,0:T(8,128)(2,1)} custom-call(bf16[512,1024]{1,0:T(8,128)(2,1)} %fusion.5.rows_ref), custom_call_target="tpu_custom_call" | custom-call | flops 1048576 | bytes 524288 | tf_op jit(solution)/shard_map/gather_tokens/pallas_call | solution.py:355
  54.6 3.7 fusion.27
  58.4 1.7 maximum_bitcast_fusion
  60.1 7.5 %fusion.23.proj_ref = f32[2048,512]{1,0:T(8,128)} fusion(bf16[2048,1024]{1,0:T(8,128)(2,1)} %gather_tokens.3, bf16[1024,768]{0,1:T(8,128)(2,1)} %all-gather.4.cloned.1.call-done), kind=kOutput, calls=%fused_computation.52 | convolution fusion | flops 2147483648 | bytes 9437184 | tf_op jit(solution)/shard_map/dot_general | solution.py:21
  67.7 12.7 %attention_forward.1 = (bf16[2048,512]{1,0:T(8,128)(2,1)S(1)}, bf16[2048,256]{1,0:T(8,128)(2,1)S(1)}, f32[16,1024]{1,0:T(8,128)S(1)}) custom-call(f32[2048,512]{1,0:T(8,128)} %fusion.23.proj_ref, f32[2048,128]{1,0:T(8,128)S(1)} %get-tuple-element.112.cosine_ref, f32[2048,128]{1,0:T(8,128)S(1)} %get-tuple-element.113.sine_ref, ...), custom_call_target="tpu_custom_call" | custom-call | flops 2147483648 | bytes 10485760 | tf_op jit(solution)/shard_map/attention_forward/pallas_call | solution.py:226
  80.4 2.7 convolution_convert_fusion.5.partial_ref
  83.2 26.5 %scatter_tokens.3 = f32[512,1024]{1,0:T(8,128)S(1)} custom-call(bf16[2048,1024]{1,0:T(8,128)(2,1)S(1)} %convolution_convert_fusion.5.partial_ref), custom_call_target="tpu_custom_call" | custom-call | flops 1048576 | bytes 524288 | tf_op jit(solution)/shard_map/scatter_tokens/pallas_call | solution.py:439
  110.1 1.3 copy-done.14
  111.4 1.2 multiply_convert_fusion.3.rows_ref
  112.6 34.3 %gather_tokens.4 = bf16[2048,1024]{1,0:T(8,128)(2,1)} custom-call(bf16[512,1024]{1,0:T(8,128)(2,1)} %multiply_convert_fusion.3.rows_ref), custom_call_target="tpu_custom_call" | custom-call | flops 1048576 | bytes 524288 | tf_op jit(solution)/shard_map/gather_tokens/pallas_call | solution.py:355
  147.0 22.5 %all-gather.6.cloned.1.call-done = bf16[1024,3456]{0,1:T(8,128)(2,1)} async-done(((bf16[128,3456]{0,1:T(8,128)(2,1)}), bf16[1024,3456]{0,1:T(8,128)(2,1)}) %all-gather.6.cloned.1.call-update) | async-done | bytes 7077904 | tf_op jit(solution)/shard_map/all_gather | solution.py:538
  169.5 10.4 %fusion.20 = f32[2048,1152]{1,0:T(8,128)} fusion(bf16[2048,1024]{1,0:T(8,128)(2,1)} %gather_tokens.4, bf16[1024,3456]{0,1:T(8,128)(2,1)} %all-gather.6.cloned.1.call-done), kind=kOutput, calls=%fused_computation.42 | convolution fusion | flops 4831838208 | bytes 15990784 | tf_op jit(solution)/shard_map/dot_general | solution.py:21
  180.0 10.6 %multiply_convert_fusion.2 = (bf16[2048,1152]{1,0:T(8,128)(2,1)S(1)}, f32[2048,1152]{1,0:T(8,128)}) fusion(f32[2048,1152]{1,0:T(8,128)} %fusion.20, bf16[2048,1024]{1,0:T(8,128)(2,1)S(1)} %copy-done.23, bf16[1024,3456]{0,1:T(8,128)(2,1)S(1)} %copy-done.32), kind=kOutput, calls=%fused_computation.2 | convolution fusion | flops 4845993984 | bytes 30146560 | tf_op jit(solution)/shard_map/dot_general | solution.py:21
  190.6 2.2 copy-done.35
  192.8 7.3 %convolution_convert_fusion.4 = bf16[2048,1024]{1,0:T(8,128)(2,1)} fusion(bf16[2048,1152]{1,0:T(8,128)(2,1)S(1)} %get-tuple-element.110, bf16[1024,3456]{0,1:T(8,128)(2,1)S(1)} %copy-done.32), kind=kOutput, calls=%fused_computation.11 | convolution fusion | flops 4833935360 | bytes 11272192 | tf_op jit(solution)/shard_map/dot_general | solution.py:31
  200.1 3.6 all-gather.8.cloned.1.call-done
  203.8 14.8 %multiply_convert_fusion = (bf16[2048,1152]{1,0:T(8,128)(2,1)S(1)}, bf16[2048,1152]{1,0:T(8,128)(2,1)S(1)}) fusion(f32[2048,1152]{1,0:T(8,128)} %fusion.20, f32[2048,1152]{1,0:T(8,128)} %get-tuple-element.111, bf16[2048,1024]{1,0:T(8,128)(2,1)} %all-gather.8.cloned.1.call-done, bf16[1024,3456]{0,1:T(8,128)(2,1)} %all-gather.6.cloned.1.call-done), kind=kOutput, calls=%fused_computation | convolution fusion | flops 4862509056 | bytes 34865152 | tf_op jit(solution)/shard_map/dot_general | solution.py:21
  218.7 11.2 %fusion.18 = f32[2048,1024]{1,0:T(8,128)} fusion(bf16[2048,1152]{1,0:T(8,128)(2,1)S(1)} %get-tuple-element.96, bf16[1024,3456]{0,1:T(8,128)(2,1)} %all-gather.6.cloned.1.call-done), kind=kOutput, calls=%fused_computation.40 | convolution fusion | flops 4831838208 | bytes 15466496 | tf_op jit(solution)/shard_map/dot_general | solution.py:31
  229.9 8.8 %add_convert_fusion.partial_ref = bf16[2048,1024]{1,0:T(8,128)(2,1)S(1)} fusion(f32[2048,1024]{1,0:T(8,128)} %fusion.18, bf16[2048,1152]{1,0:T(8,128)(2,1)S(1)} %get-tuple-element.95, bf16[1024,3456]{0,1:T(8,128)(2,1)} %all-gather.6.cloned.1.call-done), kind=kOutput, calls=%fused_computation.5 | convolution fusion | flops 4836032512 | bytes 19660800 | tf_op jit(solution)/shard_map/dot_general | solution.py:31
  238.8 33.3 %scatter_tokens.4 = f32[512,1024]{1,0:T(8,128)S(1)} custom-call(bf16[2048,1024]{1,0:T(8,128)(2,1)S(1)} %add_convert_fusion.partial_ref), custom_call_target="tpu_custom_call" | custom-call | flops 1048576 | bytes 524288 | tf_op jit(solution)/shard_map/scatter_tokens/pallas_call | solution.py:439
  272.2 6.1 %convolution_convert_fusion.1 = bf16[1024,1152]{1,0:T(8,128)(2,1)S(1)} fusion(bf16[2048,1024]{1,0:T(8,128)(2,1)S(1)} %copy-done.33, bf16[2048,1152]{1,0:T(8,128)(2,1)S(1)} %bitcast.44), kind=kOutput, calls=%fused_computation.8 | convolution fusion | flops 4833017856 | bytes 11272192 | tf_op jit(solution)/shard_map/dot_general | solution.py:25
  278.3 6.3 %convolution_convert_fusion.2 = bf16[1024,1152]{1,0:T(8,128)(2,1)S(1)} fusion(bf16[2048,1024]{1,0:T(8,128)(2,1)S(1)} %copy-done.24, bf16[2048,1152]{1,0:T(8,128)(2,1)S(1)} %bitcast.46), kind=kOutput, calls=%fused_computation.9 | convolution fusion | flops 4833017856 | bytes 11272192 | tf_op jit(solution)/shard_map/dot_general | solution.py:25
  284.6 6.1 %convolution_convert_fusion.3 = bf16[1024,1152]{1,0:T(8,128)(2,1)S(1)} fusion(bf16[2048,1024]{1,0:T(8,128)(2,1)S(1)} %copy-done.24, bf16[2048,1152]{1,0:T(8,128)(2,1)S(1)} %get-tuple-element.96), kind=kOutput, calls=%fused_computation.10 | convolution fusion | flops 4833017856 | bytes 11272192 | tf_op jit(solution)/shard_map/dot_general | solution.py:25
  290.6 3.3 pad_maximum_fusion
  294.0 2.3 multiply_reduce_fusion
  296.5 1.6 fusion.28.rows_ref
  298.1 33.4 %gather_tokens.5 = bf16[2048,1024]{1,0:T(8,128)(2,1)} custom-call(bf16[512,1024]{1,0:T(8,128)(2,1)} %fusion.28.rows_ref), custom_call_target="tpu_custom_call" | custom-call | flops 1048576 | bytes 524288 | tf_op jit(solution)/shard_map/gather_tokens/pallas_call | solution.py:355
  331.6 3.8 convolution_convert_fusion.6.grad_context_ref
  335.5 28.9 %attention_backward.1 = (bf16[2048,512]{1,0:T(8,128)(2,1)S(1)}, f32[16,384]{1,0:T(8,128)S(1)}) custom-call(f32[2048,512]{1,0:T(8,128)} %fusion.23.proj_ref, f32[2048,128]{1,0:T(8,128)S(1)} %copy-done.2, f32[2048,128]{1,0:T(8,128)S(1)} %copy-done.4, f32[1,256]{1,0:T(1,128)S(1)} %copy-done.9, f32[1,128]{1,0:T(1,128)S(1)} %copy-done.11, ...), custom_call_target="tpu_custom_call" | custom-call | flops 2097152 | bytes 1048576 | tf_op jit(solution)/shard_map/attention_backward/pallas_call | solution.py:258
  364.4 1.3 copy-done.12
  366.0 3.6 convolution_convert_fusion.8
  370.2 2.4 convolution_convert_fusion.7
  372.6 1.3 pad_maximum_fusion.1
  374.0 49.2 %reduce-scatter.8.cloned.1.call-done = bf16[128,3456]{1,0:T(8,128)(2,1)} async-done(((bf16[1024,3456]{1,0:T(8,128)(2,1)}), bf16[128,3456]{1,0:T(8,128)(2,1)}) %reduce-scatter.8.cloned.1.call-update) | async-done | bytes 884752 | tf_op jit(solution)/shard_map/reduce_scatter | solution.py:588
  423.1 2.6 copy.64
  425.8 4.2 convolution_convert_fusion.partial_ref
  430.0 27.3 %scatter_tokens.5 = f32[512,1024]{1,0:T(8,128)S(1)} custom-call(bf16[2048,1024]{1,0:T(8,128)(2,1)S(1)} %convolution_convert_fusion.partial_ref), custom_call_target="tpu_custom_call" | custom-call | flops 1048576 | bytes 524288 | tf_op jit(solution)/shard_map/scatter_tokens/pallas_call | solution.py:439
  457.3 1.3 copy-done
  460.0 9.9 %sum_gains.1 = f32[24,128]{1,0:T(8,128)} custom-call(f32[24,128]{1,0:T(8,128)} %pad_bitcast_fusion.part_ref), custom_call_target="tpu_custom_call" | custom-call | tf_op jit(solution)/shard_map/sum_gains/pallas_call | solution.py:497
  471.2 1.3 slice_bitcast_fusion.3
  472.5 4.6 fusion.9
  478.3 1.1 fusion.29
  479.4 11.2 %reduce-scatter.10.cloned.1.call-done = bf16[128,768]{1,0:T(8,128)(2,1)} async-done(((bf16[1024,768]{1,0:T(8,128)(2,1)}), bf16[128,768]{1,0:T(8,128)(2,1)}) %reduce-scatter.10.cloned.1.call-update) | async-done | bytes 196624
  (132 shorter events, 13.6 us)
Async XLA Ops:
  7.2 9.6 %copy-start.34 = (f32[64]{0:T(128)S(1)}, f32[64]{0:T(128)}, u32[]{:S(2)}) copy-start(f32[64]{0:T(128)} %param.21) | copy-start | bytes 772
  7.2 9.7 %copy-start.31 = (f32[64]{0:T(128)S(1)}, f32[64]{0:T(128)}, u32[]{:S(2)}) copy-start(f32[64]{0:T(128)} %param.20) | copy-start | bytes 772
  7.2 9.8 %copy-start.16 = (bf16[512,1024]{1,0:T(8,128)(2,1)S(1)}, bf16[512,1024]{1,0:T(8,128)(2,1)}, u32[]{:S(2)}) copy-start(bf16[512,1024]{1,0:T(8,128)(2,1)} %param.14) | copy-start | bytes 3145732
  7.2 10.1 %copy-start.30 = (s32[2048]{0:T(1024)S(1)}, s32[2048]{0:T(1024)}, u32[]{:S(2)}) copy-start(s32[2048]{0:T(1024)} %param.15) | copy-start | bytes 24580
  7.2 10.1 %copy-start.26 = (f32[1024]{0:T(1024)S(1)}, f32[1024]{0:T(1024)}, u32[]{:S(2)}) copy-start(f32[1024]{0:T(1024)} %param.16) | copy-start | bytes 12292
  7.2 52.9 %all-gather.4.cloned.1.call-start = ((), (), s32[]{:S(2)}) async-start(), calls=%async_computation.3 | async-start | bytes 1769472 | tf_op jit(solution)/shard_map/all_gather | solution.py:534
  11.6 157.9 %all-gather.6.cloned.1.call-start = ((), (), s32[]{:S(2)}) async-start(), calls=%async_computation.4 | async-start | bytes 7962624 | tf_op jit(solution)/shard_map/all_gather | solution.py:538
  16.0 187.8 %all-gather.8.cloned.1.call-start = ((), (), s32[]{:S(2)}) async-start(), calls=%async_computation.5 | async-start | bytes 5242880 | tf_op jit(solution)/shard_map/all_gather | solution.py:559
  16.7 277.2 %reduce-scatter.6.cloned.1.call-start = ((), (), s32[]{:S(2)}) async-start(), calls=%async_computation.6 | async-start | bytes 5242880 | tf_op jit(solution)/shard_map/reduce_scatter | solution.py:575
  16.9 50.8 %copy-start.10 = (f32[1,128]{1,0:T(1,128)}, f32[1,128]{1,0:T(1,128)S(1)}, u32[]{:S(2)}) copy-start(f32[1,128]{1,0:T(1,128)S(1)} %broadcast_in_dim_tile.7.key_gain_ref) | copy-start | bytes 1540
  17.0 50.7 %copy-start.8 = (f32[1,256]{1,0:T(1,128)}, f32[1,256]{1,0:T(1,128)S(1)}, u32[]{:S(2)}) copy-start(f32[1,256]{1,0:T(1,128)S(1)} %broadcast_in_dim_tile.6.query_gain_ref) | copy-start | bytes 3076
  17.3 1.3 copy-start.28
  60.0 7.6 %copy-start.1 = (f32[2048,128]{1,0:T(8,128)}, f32[2048,128]{1,0:T(8,128)S(1)}, u32[]{:S(2)}) copy-start(f32[2048,128]{1,0:T(8,128)S(1)} %get-tuple-element.112.cosine_ref) | copy-start | bytes 3145732
  60.1 7.6 %copy-start.3 = (f32[2048,128]{1,0:T(8,128)}, f32[2048,128]{1,0:T(8,128)S(1)}, u32[]{:S(2)}) copy-start(f32[2048,128]{1,0:T(8,128)S(1)} %get-tuple-element.113.sine_ref) | copy-start | bytes 3145732
  80.4 2.7 copy-start.5
  80.4 2.7 copy-start.7
  83.1 26.5 %copy-start.17 = (bf16[512,1024]{1,0:T(8,128)(2,1)S(1)}, bf16[512,1024]{1,0:T(8,128)(2,1)}, u32[]{:S(2)}) copy-start(bf16[512,1024]{1,0:T(8,128)(2,1)} %param.14) | copy-start | bytes 3145732
  109.7 1.7 copy-start.25
  110.0 1.4 copy-start.14
  169.5 10.4 %copy-start.23 = (bf16[2048,1024]{1,0:T(8,128)(2,1)S(1)}, bf16[2048,1024]{1,0:T(8,128)(2,1)}, u32[]{:S(2)}) copy-start(bf16[2048,1024]{1,0:T(8,128)(2,1)} %gather_tokens.4) | copy-start | bytes 12582916
  169.5 10.4 %copy-start.32 = (bf16[1024,3456]{0,1:T(8,128)(2,1)S(1)}, bf16[1024,3456]{0,1:T(8,128)(2,1)}, u32[]{:S(2)}) copy-start(bf16[1024,3456]{0,1:T(8,128)(2,1)} %all-gather.6.cloned.1.call-done) | copy-start | bytes 21233668
  190.6 2.2 copy-start.35
  203.8 219.3 %reduce-scatter.8.cloned.1.call-start = ((), (), s32[]{:S(2)}) async-start(), calls=%async_computation.7 | async-start | bytes 7962624 | tf_op jit(solution)/shard_map/reduce_scatter | solution.py:588
  218.7 11.3 %copy-start.36 = (bf16[2048,1152]{1,0:T(8,128)(2,1)}, bf16[2048,1152]{1,0:T(8,128)(2,1)S(1)}, u32[]{:S(2)}) copy-start(bf16[2048,1152]{1,0:T(8,128)(2,1)S(1)} %get-tuple-element.95) | copy-start | bytes 14155780
  218.7 53.4 %slice-start = ((s8[4718592]{0:T(1024)(128)(4,1)}), s8[4194304]{0:T(1024)(128)(4,1)S(1)}, s32[]{:S(2)}) async-start(s8[4718592]{0:T(1024)(128)(4,1)} %bitcast.43), calls=%async_computation.9 | async-start | bytes 8388608
  229.9 42.2 %slice-start.1 = ((s8[4718592]{0:T(1024)(128)(4,1)}), s8[524288]{0:T(1024)(128)(4,1)S(1)}, s32[]{:S(2)}) async-start(s8[4718592]{0:T(1024)(128)(4,1)} %bitcast.43), calls=%async_computation.10 | async-start | bytes 1048576
  238.8 33.4 %copy-start.33 = (bf16[2048,1024]{1,0:T(8,128)(2,1)S(1)}, bf16[2048,1024]{1,0:T(8,128)(2,1)}, u32[]{:S(2)}) copy-start(bf16[2048,1024]{1,0:T(8,128)(2,1)} %all-gather.8.cloned.1.call-done) | copy-start | bytes 12582916
  238.8 39.5 %slice-start.2 = ((s8[4718592]{0:T(1024)(128)(4,1)}), s8[4194304]{0:T(1024)(128)(4,1)S(1)}, s32[]{:S(2)}) async-start(s8[4718592]{0:T(1024)(128)(4,1)} %bitcast.45), calls=%async_computation.11 | async-start | bytes 8388608
  272.1 6.1 %copy-start.24 = (bf16[2048,1024]{1,0:T(8,128)(2,1)S(1)}, bf16[2048,1024]{1,0:T(8,128)(2,1)}, u32[]{:S(2)}) copy-start(bf16[2048,1024]{1,0:T(8,128)(2,1)} %gather_tokens.4) | copy-start | bytes 12582916
  272.2 6.1 %slice-start.3 = ((s8[4718592]{0:T(1024)(128)(4,1)}), s8[524288]{0:T(1024)(128)(4,1)S(1)}, s32[]{:S(2)}) async-start(s8[4718592]{0:T(1024)(128)(4,1)} %bitcast.45), calls=%async_computation.12 | async-start | bytes 1048576
  293.9 2.4 copy-start.19
  294.0 196.6 %reduce-scatter.10.cloned.1.call-start = ((), (), s32[]{:S(2)}) async-start(), calls=%async_computation.8 | async-start | bytes 1769472
  294.0 2.5 copy-start.15
  331.6 3.9 copy-start.2
  331.6 3.9 copy-start.4
  331.6 3.9 copy-start.9
  331.6 3.9 copy-start.11
  335.5 30.5 %copy-start.6 = (bf16[2048,256]{1,0:T(8,128)(2,1)S(1)}, bf16[2048,256]{1,0:T(8,128)(2,1)}, u32[]{:S(2)}) copy-start(bf16[2048,256]{1,0:T(8,128)(2,1)} %copy-done.5) | copy-start | bytes 3145732
  364.4 1.3 copy-start.12
  366.0 3.7 copy-start.13
  366.0 4.2 copy-start.22
  430.0 28.7 %copy-start.18 = (bf16[512,1024]{1,0:T(8,128)(2,1)S(1)}, bf16[512,1024]{1,0:T(8,128)(2,1)}, u32[]{:S(2)}) copy-start(bf16[512,1024]{1,0:T(8,128)(2,1)} %param.14) | copy-start | bytes 3145732
  430.0 28.6 %copy-start.27 = (f32[1024]{0:T(1024)S(1)}, f32[1024]{0:T(1024)}, u32[]{:S(2)}) copy-start(f32[1024]{0:T(1024)} %param.16) | copy-start | bytes 12292
  430.0 28.6 %copy-start.29 = (f32[512]{0:T(512)S(1)}, f32[512]{0:T(512)}, u32[]{:S(2)}) copy-start(f32[512]{0:T(512)} %copy-done.28) | copy-start | bytes 6148
  457.3 1.3 copy-start
  472.5 4.6 copy-start.20
  477.1 1.2 copy-start.21
Sparse Core Ops, SparseCore 0:
  11.7 47.9 all-gather.3
  61.8 107.6 all-gather.5
  171.1 32.6 all-gather.7
  206.1 50.7 reduce-scatter.5
  294.1 129.0 reduce-scatter.7
  426.4 64.1 reduce-scatter.9
